TPU v7x, 32 devices: a whole 2x2x4 slice. The times are simulated.
32 devices in a mesh: dp: 8 (over y, x, core), tensor: 4 (over z).
Axes of the slice: x: 2, y: 2, z: 4, core: 2. Of those that a mesh axis runs over, the one named last changes fastest.
Arguments:
- block_input: bfloat16 [4096, 1536], P('dp'), may hold values from -6 to 6
- seq_lengths: int32 [2], replicated, may hold values from 1024 to 2048, as said below
- pre_gain: float32 [1536], replicated, may hold values from 0.5 to 1.5
- gate_weight: bfloat16 [1536, 3072], P(None, 'tensor'), may hold values from -0.15625 to 0.15625
- value_weight: bfloat16 [1536, 3072], P(None, 'tensor'), may hold values from -0.15625 to 0.15625
- state_proj: bfloat16 [1536, 256], replicated, may hold values from -0.15625 to 0.15625
- step_weight: bfloat16 [1536, 48], P(None, 'tensor'), may hold values from -0.15625 to 0.15625
- conv_weight: float32 [4, 3072], P(None, 'tensor'), may hold values from -3 to 3
- conv_bias: float32 [3072], P('tensor'), may hold values from -1.5 to 1.5
- state_conv_weight: float32 [4, 256], replicated, may hold values from -3 to 3
- state_conv_bias: float32 [256], replicated, may hold values from -1.5 to 1.5
- step_bias: float32 [48], P('tensor'), may hold values from -3 to 0
- decay_log: float32 [48], P('tensor'), may hold values from -8 to 0.5
- skip_gain: float32 [48], P('tensor'), may hold values from 0.5 to 1.5
- norm_gain: float32 [3072], P('tensor'), may hold values from 0.5 to 1.5
- out_weight: bfloat16 [3072, 1536], P('tensor'), may hold values from -0.109375 to 0.109375
- out_grad: bfloat16 [4096, 1536], P('dp'), may hold values from -6 to 6
Outputs:
- block_output: bfloat16 [4096, 1536], P('dp')
- input_grad: bfloat16 [4096, 1536], P('dp')
- pre_gain_grad: float32 [1536], P('dp')
- gate_weight_grad: float32 [1536, 3072], P('dp', 'tensor')
- value_weight_grad: float32 [1536, 3072], P('dp', 'tensor')
- state_proj_grad: float32 [1536, 256], P('dp')
- step_weight_grad: float32 [1536, 48], P('dp', 'tensor')
- conv_weight_grad: float32 [4, 3072], P(None, 'tensor')
- conv_bias_grad: float32 [3072], P('tensor')
- state_conv_weight_grad: float32 [4, 256], replicated
- state_conv_bias_grad: float32 [256], replicated
- step_bias_grad: float32 [48], P('tensor')
- decay_log_grad: float32 [48], P('tensor')
- skip_gain_grad: float32 [48], P('tensor')
- norm_gain_grad: float32 [3072], P('tensor')
- out_weight_grad: float32 [3072, 1536], P('tensor', 'dp')
Inputs may be any that keep to these rules, and one draw needn't show every extreme that they name: `seq_lengths`: 2 lengths of the sequences packed one after another over all 4096 tokens, in order; they sum to 4096 and one of them is exactly 2048.
All inputs are finite; a program needn't handle non-finite values.
Results may differ from a plain program's by a relative error of at most 0.015.
Values may be sent and summed in bfloat16 or wider, within the bound.
A program may use at most 128 MiB of HBM per device.

v0:
```python
import jax
import jax.numpy as jnp
from jax import lax
from jax.sharding import PartitionSpec as P

HEADS = 48
HEADDIM = 64
BLOCK = 256


epsilon = 1e-05


def from_behind(value, axis, steps):
    count = lax.axis_size(axis)
    initial, last = (max(0, -steps), min(count, count - steps))
    return lax.ppermute(value, axis, [(source, source + steps) for source in range(initial, last)])


def carried_in(part, axis, combine, identity, reverse):
    count = lax.axis_size(axis)
    place = lax.axis_index(axis)
    ahead = count - 1 - place if reverse else place
    gathered = jax.tree.map(lambda a: lax.all_gather(a, axis), part)
    state = jax.tree.map(lambda a, e: jnp.zeros_like(a) + jnp.asarray(e, a.dtype), part, identity)

    def one(lap, state):
        source = count - 1 - lap if reverse else lap
        return combine(
            state, jax.tree.map(lambda a: lax.dynamic_index_in_dim(a, source, 0, False), gathered)
        )

    return lax.fori_loop(0, ahead, one, state)


def positions(seq_lengths, first_token, tok_count):
    tokens_at = first_token + jnp.arange(tok_count, dtype=jnp.int32)
    starts = jnp.cumsum(seq_lengths) - seq_lengths
    before = starts[None, :] <= tokens_at[:, None]
    seq_ids = jnp.sum(before.astype(jnp.int32), axis=1) - 1
    seq_start = jnp.max(jnp.where(before, starts[None, :], 0), axis=1)
    return (seq_ids, tokens_at - seq_start)


def matmul(left, right):
    return jnp.dot(left, right, preferred_element_type=jnp.float32)


def matmul_rt(left, right):
    return lax.dot_general(
        left, right, (((1,), (1,)), ((), ())), preferred_element_type=jnp.float32
    )


def matmul_lt(left, right):
    return lax.dot_general(
        left, right, (((0,), (0,)), ((), ())), preferred_element_type=jnp.float32
    )


def exact(form, left, right):
    return jnp.einsum(form, left, right, precision=lax.Precision.HIGHEST)


def silu_grad(value):
    sigma = jax.nn.sigmoid(value)
    return sigma * (1.0 + value * (1.0 - sigma))


def conv_apply(extended, weight, offset, seq_place, tok_count):
    tap_count = weight.shape[0]
    running_sum = jnp.zeros((tok_count, weight.shape[1]), jnp.float32) + offset
    for tap_index in range(tap_count):
        valid_tap = (seq_place >= tap_count - 1 - tap_index).astype(jnp.float32)[:, None]
        running_sum = (
            running_sum
            + weight[tap_index] * extended[tap_index : tap_index + tok_count] * valid_tap
        )
    return running_sum


def conv_back(extended, weight, grad_pre, seq_place, tok_count):
    tap_count = weight.shape[0]
    weight_rows = []
    grad_ext = jnp.zeros(extended.shape, jnp.float32)
    for tap_index in range(tap_count):
        valid_tap = (seq_place >= tap_count - 1 - tap_index).astype(jnp.float32)[:, None]
        masked = grad_pre * valid_tap
        weight_rows.append(jnp.sum(masked * extended[tap_index : tap_index + tok_count], axis=0))
        grad_ext = grad_ext.at[tap_index : tap_index + tok_count].add(weight[tap_index] * masked)
    return (jnp.stack(weight_rows), jnp.sum(grad_pre, axis=0), grad_ext)


def chain_state(running, element):
    factor_now, block_end = element
    return (factor_now[:, None, None] * running + block_end, running)


def back_chain(running, element):
    factor_now, grad_part = element
    return (grad_part + factor_now[:, None, None] * running, running)


def combine_fwd(earlier, later):
    return (earlier[0] * later[0], later[0][:, None, None] * earlier[1] + later[1])


def combine_back(earlier, later):
    return (earlier[0] * later[0], later[1] + later[0][:, None, None] * earlier[1])


def norm_back_rows(grad_rows, input_rows, inv_rows, pre_gain):
    gain_part = jnp.sum(grad_rows * input_rows * inv_rows, axis=0)
    scaled = grad_rows * pre_gain
    result = inv_rows * scaled - input_rows * inv_rows**3 * jnp.mean(
        scaled * input_rows, axis=1, keepdims=True
    )
    return (gain_part, result)


def on_device(
    block_input,
    seq_lengths,
    pre_gain,
    gate_weight,
    value_weight,
    state_proj,
    step_weight,
    conv_weight,
    conv_bias,
    state_conv_weight,
    state_conv_bias,
    step_bias,
    decay_log,
    skip_gain,
    norm_gain,
    out_weight,
    out_grad,
):
    tok_count = block_input.shape[0]
    head_count = step_weight.shape[1]
    inner_width = gate_weight.shape[1]
    head_dim = inner_width // head_count
    state_dim = state_proj.shape[1] // 2
    tap_count = conv_weight.shape[0]
    blocks = tok_count // BLOCK
    seq_ids, seq_place = positions(seq_lengths, lax.axis_index("dp") * tok_count, tok_count)
    resets = (seq_place == 0).astype(jnp.float32)
    inputs = block_input.astype(jnp.float32)
    inv_in = lax.rsqrt(jnp.mean(inputs * inputs, axis=1, keepdims=True) + epsilon)
    normed_in = (inputs * inv_in * pre_gain).astype(jnp.bfloat16)
    gate_proj = matmul(normed_in, gate_weight).astype(jnp.bfloat16)
    values_raw = matmul(normed_in, value_weight).astype(jnp.bfloat16)
    state_raw = matmul(normed_in, state_proj).astype(jnp.bfloat16)
    step_raw = matmul(normed_in, step_weight).astype(jnp.bfloat16)
    tails = from_behind(
        (values_raw[tok_count - tap_count + 1 :], state_raw[tok_count - tap_count + 1 :]), "dp", 1
    )
    value_ext = jnp.concatenate([tails[0], values_raw], axis=0).astype(jnp.float32)
    state_ext = jnp.concatenate([tails[1], state_raw], axis=0).astype(jnp.float32)
    value_pre = conv_apply(value_ext, conv_weight, conv_bias, seq_place, tok_count)
    state_pre = conv_apply(state_ext, state_conv_weight, state_conv_bias, seq_place, tok_count)
    values = jax.nn.silu(value_pre).astype(jnp.bfloat16)
    states = jax.nn.silu(state_pre).astype(jnp.bfloat16)
    step_pre = step_raw.astype(jnp.float32) + step_bias
    step_sizes = jax.nn.softplus(step_pre)
    decay_rates = -jnp.exp(decay_log)
    logdec = step_sizes * decay_rates
    head_values = values.astype(jnp.float32).reshape(blocks, BLOCK, head_count, head_dim)
    step_blocks = step_sizes.reshape(blocks, BLOCK, head_count)
    weighted = head_values * step_blocks[..., None]
    states_f = states.astype(jnp.float32)
    input_mat = states_f[:, :state_dim].reshape(blocks, BLOCK, state_dim)
    output_mat = states_f[:, state_dim:].reshape(blocks, BLOCK, state_dim)
    input_low = states[:, :state_dim].reshape(blocks, BLOCK, state_dim)
    output_low = states[:, state_dim:].reshape(blocks, BLOCK, state_dim)
    cum_log = jnp.cumsum(logdec.reshape(blocks, BLOCK, head_count), axis=1)
    seq_blocks = seq_ids.reshape(blocks, BLOCK)
    causal = jnp.arange(BLOCK)[:, None] >= jnp.arange(BLOCK)[None, :]
    same_seq = ((seq_blocks[:, :, None] == seq_blocks[:, None, :]) & causal[None])[:, None]
    cum_heads = jnp.swapaxes(cum_log, 1, 2)
    log_gap = cum_heads[:, :, :, None] - cum_heads[:, :, None, :]
    decay_mask = jnp.where(same_seq, jnp.exp(jnp.where(same_seq, log_gap, 0.0)), 0.0)
    scores = jnp.einsum("ctn,csn->cts", output_low, input_low, preferred_element_type=jnp.float32)
    mixed_scores = decay_mask * scores[:, None]
    within_block = exact("chts,cshp->cthp", mixed_scores, weighted)
    keep_mask = jnp.cumprod(1.0 - resets.reshape(blocks, BLOCK), axis=1)
    carried = keep_mask[..., None] * jnp.exp(cum_log)
    factor = carried[:, -1]
    last_same = (seq_blocks == seq_blocks[:, -1:]).astype(jnp.float32)
    tail_weight = last_same[..., None] * jnp.exp(cum_log[:, -1:] - cum_log)
    block_ends = exact("cshp,csn->chpn", tail_weight[..., None] * weighted, input_mat)
    zero_state = jnp.zeros((head_count, head_dim, state_dim), jnp.float32)
    local_end, unused = lax.scan(chain_state, zero_state, (factor, block_ends))
    dev_factor = jnp.prod(factor, axis=0)
    incoming = carried_in(
        (dev_factor, local_end), "dp", combine_fwd, (jnp.ones_like(dev_factor), zero_state), False
    )[1]
    unused, starts_state = lax.scan(chain_state, incoming, (factor, block_ends))
    projected = exact("chpn,ctn->cthp", starts_state, output_mat)
    ssd_out = within_block + carried[..., None] * projected + skip_gain[:, None] * head_values
    mixer_out = ssd_out.reshape(tok_count, inner_width)
    gate_f = gate_proj.astype(jnp.float32)
    gate_act = jax.nn.silu(gate_f)
    gated_out = mixer_out * gate_act
    variance = lax.psum(jnp.sum(gated_out * gated_out, axis=1), "tensor") / (HEADS * HEADDIM)
    inv_out = lax.rsqrt(variance + epsilon)[:, None]
    normed = (gated_out * inv_out * norm_gain).astype(jnp.bfloat16)
    share_rows = tok_count // lax.axis_size("tensor")
    share_sum = lax.psum_scatter(
        matmul(normed, out_weight), "tensor", scatter_dimension=0, tiled=True
    )
    own_rows = lax.dynamic_slice_in_dim(
        inputs, lax.axis_index("tensor") * share_rows, share_rows, 0
    )
    block_output = lax.all_gather(
        (own_rows + share_sum).astype(jnp.bfloat16), "tensor", axis=0, tiled=True
    )
    grad_out_f = out_grad.astype(jnp.float32)
    grad_normed = matmul_rt(out_grad, out_weight)
    out_weight_g = matmul_lt(normed, out_grad)
    norm_gain_g = jnp.sum(grad_normed * gated_out * inv_out, axis=0)
    grad_scaled = grad_normed * norm_gain
    cross_sum = lax.psum(jnp.sum(grad_scaled * gated_out, axis=1), "tensor") / (HEADS * HEADDIM)
    grad_gated = inv_out * grad_scaled - gated_out * inv_out**3 * cross_sum[:, None]
    grad_mixer = grad_gated * gate_act
    grad_gate = (grad_gated * mixer_out * silu_grad(gate_f)).astype(jnp.bfloat16)
    grad_blocks = grad_mixer.reshape(blocks, BLOCK, head_count, head_dim)
    skip_g = jnp.sum(grad_blocks * head_values, axis=(0, 1, 3))
    grad_values = skip_gain[:, None] * grad_blocks
    grad_carried = jnp.sum(grad_blocks * projected, axis=3)
    grad_cum = grad_carried * carried
    scaled_grad = carried[..., None] * grad_blocks
    state_grads_local = exact("cthp,ctn->chpn", scaled_grad, output_mat)
    grad_output_mat = exact("cthp,chpn->ctn", scaled_grad, starts_state)
    dev_grad, unused = lax.scan(back_chain, zero_state, (factor, state_grads_local), reverse=True)
    outgoing = carried_in(
        (dev_factor, dev_grad), "dp", combine_back, (jnp.ones_like(dev_factor), zero_state), True
    )[1]
    unused, end_grads = lax.scan(back_chain, outgoing, (factor, state_grads_local), reverse=True)
    grad_factor = jnp.sum(end_grads * starts_state, axis=(2, 3))
    through = exact("chpn,csn->cshp", end_grads, input_mat)
    grad_weighted = tail_weight[..., None] * through
    grad_tail = jnp.sum(weighted * through, axis=3) * tail_weight
    grad_cum = grad_cum - grad_tail
    grad_cum = grad_cum.at[:, -1].add(grad_factor * factor + jnp.sum(grad_tail, axis=1))
    grad_input_mat = exact("cshp,chpn->csn", tail_weight[..., None] * weighted, end_grads)
    grad_mixed = exact("cthp,cshp->chts", grad_blocks, weighted)
    grad_weighted = grad_weighted + exact("chts,cthp->cshp", mixed_scores, grad_blocks)
    grad_scores = jnp.sum(grad_mixed * decay_mask, axis=1)
    grad_gap = grad_mixed * mixed_scores
    grad_cum = (
        grad_cum
        + jnp.swapaxes(jnp.sum(grad_gap, axis=3), 1, 2)
        - jnp.swapaxes(jnp.sum(grad_gap, axis=2), 1, 2)
    )
    grad_output_mat = grad_output_mat + exact("cts,csn->ctn", grad_scores, input_mat)
    grad_input_mat = grad_input_mat + exact("cts,ctn->csn", grad_scores, output_mat)
    grad_logdec = jnp.flip(jnp.cumsum(jnp.flip(grad_cum, 1), axis=1), 1).reshape(
        tok_count, head_count
    )
    grad_values = grad_values + grad_weighted * step_blocks[..., None]
    grad_steps = grad_logdec * decay_rates + jnp.sum(grad_weighted * head_values, axis=3).reshape(
        tok_count, head_count
    )
    decay_log_g = jnp.sum(grad_logdec * step_sizes, axis=0) * decay_rates
    grad_step_pre = grad_steps * jax.nn.sigmoid(step_pre)
    step_bias_g = jnp.sum(grad_step_pre, axis=0)
    grad_states = lax.psum(
        jnp.concatenate(
            [
                grad_input_mat.reshape(tok_count, state_dim),
                grad_output_mat.reshape(tok_count, state_dim),
            ],
            axis=1,
        ),
        "tensor",
    )
    grad_value_pre = grad_values.reshape(tok_count, inner_width) * silu_grad(value_pre)
    grad_state_pre = grad_states * silu_grad(state_pre)
    conv_g, conv_bias_g, grad_value_ext = conv_back(
        value_ext, conv_weight, grad_value_pre, seq_place, tok_count
    )
    state_conv_g, state_conv_bias_g, grad_state_ext = conv_back(
        state_ext, state_conv_weight, grad_state_pre, seq_place, tok_count
    )
    heads_back = from_behind(
        (grad_value_ext[: tap_count - 1], grad_state_ext[: tap_count - 1]), "dp", -1
    )
    lead_rows = tok_count - tap_count + 1
    grad_values_raw = grad_value_ext[tap_count - 1 :] + jnp.concatenate(
        [jnp.zeros((lead_rows, inner_width), jnp.float32), heads_back[0]], axis=0
    )
    grad_state_raw = grad_state_ext[tap_count - 1 :] + jnp.concatenate(
        [jnp.zeros((lead_rows, 2 * state_dim), jnp.float32), heads_back[1]], axis=0
    )
    grad_values_low = grad_values_raw.astype(jnp.bfloat16)
    grad_state_low = grad_state_raw.astype(jnp.bfloat16)
    grad_step_low = grad_step_pre.astype(jnp.bfloat16)
    gate_g = matmul_lt(normed_in, grad_gate)
    value_g = matmul_lt(normed_in, grad_values_low)
    state_g = matmul_lt(normed_in, grad_state_low)
    step_g = matmul_lt(normed_in, grad_step_low)
    partial_in = (
        matmul_rt(grad_gate, gate_weight)
        + matmul_rt(grad_values_low, value_weight)
        + matmul_rt(grad_step_low, step_weight)
    )
    grad_normed_in = lax.psum(partial_in, "tensor") + matmul_rt(grad_state_low, state_proj)
    pre_gain_g, grad_inputs = norm_back_rows(grad_normed_in, inputs, inv_in, pre_gain)
    input_grad = (grad_out_f + grad_inputs).astype(jnp.bfloat16)
    summed = (
        lax.psum_scatter(pre_gain_g, "dp", scatter_dimension=0, tiled=True),
        lax.psum_scatter(gate_g, "dp", scatter_dimension=0, tiled=True),
        lax.psum_scatter(value_g, "dp", scatter_dimension=0, tiled=True),
        lax.psum_scatter(state_g, "dp", scatter_dimension=0, tiled=True),
        lax.psum_scatter(step_g, "dp", scatter_dimension=0, tiled=True),
        lax.psum_scatter(out_weight_g, "dp", scatter_dimension=1, tiled=True),
    )
    smalls = lax.psum(
        (
            conv_g,
            conv_bias_g,
            state_conv_g,
            state_conv_bias_g,
            step_bias_g,
            decay_log_g,
            skip_g,
            norm_gain_g,
        ),
        "dp",
    )
    return (
        block_output,
        input_grad,
        summed[0],
        summed[1],
        summed[2],
        summed[3],
        summed[4],
        smalls[0],
        smalls[1],
        smalls[2],
        smalls[3],
        smalls[4],
        smalls[5],
        smalls[6],
        smalls[7],
        summed[5],
    )


def solution(mesh):
    in_specs = (
        P("dp", None),
        P(),
        P(),
        P(None, "tensor"),
        P(None, "tensor"),
        P(),
        P(None, "tensor"),
        P(None, "tensor"),
        P("tensor"),
        P(),
        P(),
        P("tensor"),
        P("tensor"),
        P("tensor"),
        P("tensor"),
        P("tensor", None),
        P("dp", None),
    )
    out_specs = (
        P("dp", None),
        P("dp", None),
        P("dp"),
        P("dp", "tensor"),
        P("dp", "tensor"),
        P("dp", None),
        P("dp", "tensor"),
        P(None, "tensor"),
        P("tensor"),
        P(),
        P(),
        P("tensor"),
        P("tensor"),
        P("tensor"),
        P("tensor"),
        P("tensor", "dp"),
    )
    return jax.shard_map(
        on_device, mesh=mesh, in_specs=in_specs, out_specs=out_specs, check_vma=False
    )
```

profile of v0, /device:TPU:0, one launch (start us, length us, event | category | flops | bytes accessed | tf_op | source)
XLA Modules:
  0.0 712.2 jit_solution(13982719997441013845)
XLA Ops:
  61.0 11.9 %all-reduce.4 = f32[96]{0:T(128)S(1)} all-reduce(f32[96]{0:T(128)S(1)} %dynamic-update-slice.27), channel_id=2, replica_groups=mesh['dp'=8,'tensor'=4] {'dp'}, use_global_device_ids=true, to_apply=%add.4 | all-reduce | flops 96 | bytes 768
  76.2 11.2 %all-gather.9.cloned.1.call-done = f32[96,64,128]{2,1,0:T(8,128)} async-done(((f32[12,64,128]{2,1,0:T(8,128)}), f32[96,64,128]{2,1,0:T(8,128)}) %all-gather.9.cloned.1.call-update) | async-done | bytes 3145744 | tf_op jit(solution)/shard_map/all_gather | solution.py:24
  88.6 5.1 while.90
  95.9 7.2 %fusion.39 = f32[2,256,12,64]{1,3,2,0:T(8,128)S(1)} fusion(f32[2,256,12,64]{1,3,2,0:T(8,128)S(1)} %fusion.118, f32[2,256,256]{2,1,0:T(8,128)S(1)} %copy-done.43, f32[2,12,256]{2,1,0:T(8,128)S(1)} %copy-done.70, pred[2,256,256]{2,1,0:T(8,128)(4,1)S(1)} %copy-done.53, f32[2,256,12,64]{1,0,3,2:T(2,128)S(1)} %copy-done.13, f32[12]{0:T(128)S(1)} %copy-done.100, ...), kind=kOutput, calls=%fused_computation.70 | convolution fusion | flops 1216217088 | bytes 5447728 | tf_op jit(solution)/shard_map/chts,cshp->cthp/dot_general | solution.py:62
  108.7 5.1 multiply_reduce_fusion.11
  113.8 11.7 %psum.84 = f32[512]{0:T(512)S(1)} all-reduce(f32[512]{0:T(512)S(1)} %get-tuple-element.655), channel_id=1, replica_groups=mesh['dp'=8,'tensor'=4] {'tensor'}, use_global_device_ids=true, to_apply=%region_16.17 | all-reduce | flops 512 | bytes 4096 | tf_op jit(solution)/shard_map/psum | solution.py:206
  125.5 5.5 multiply_reduce_fusion.1
  131.0 8.5 %psum.85 = f32[512]{0:T(512)S(1)} all-reduce(f32[512]{0:T(512)S(1)} %get-tuple-element.530), channel_id=1, replica_groups=mesh['dp'=8,'tensor'=4] {'tensor'}, use_global_device_ids=true, to_apply=%region_19.20 | all-reduce | flops 512 | bytes 4096 | tf_op jit(solution)/shard_map/psum | solution.py:224
  139.6 5.0 multiply_reduce_fusion.2
  159.3 11.9 %fusion.9 = (f32[2,12,256]{2,1,0:T(8,128)S(1)}, f32[2,12,256]{2,1,0:T(8,128)S(1)}, f32[2,256,256]{2,1,0:T(8,128)}) fusion(f32[2,256,256]{2,1,0:T(8,128)} %fusion.117, f32[2,12,256]{2,1,0:T(8,128)} %copy.207, pred[2,256,256]{2,1,0:T(8,128)(4,1)} %compare_and_fusion, f32[2,256,12,64]{1,0,3,2:T(2,128)} %reshape.504, f32[2,256,12]{1,2,0:T(8,128)} %copy.203, ...), kind=kOutput, calls=%fused_computation.25 | convolution fusion | flops 1222365184 | bytes 4423680 | tf_op jit(solution)/shard_map/cthp,cshp->chts/dot_general | solution.py:62
  185.1 16.3 %all-gather.11.cloned.1.call-done = f32[96,64,128]{2,1,0:T(8,128)} async-done(((f32[12,64,128]{2,1,0:T(8,128)}), f32[96,64,128]{2,1,0:T(8,128)}) %all-gather.11.cloned.1.call-update) | async-done | bytes 3145744 | tf_op jit(solution)/shard_map/all_gather | solution.py:24
  201.5 13.5 %while.91 = (s32[]{:T(128)}, f32[12,64,128]{2,1,0:T(8,128)S(1)}, s32[]{:T(128)}, f32[8,12,64,128]{3,2,1,0:T(8,128)}, f32[8,12]{1,0:T(8,128)}, /*index=5*/s32[]{:T(128)}, s32[]{:T(128)}, s32[]{:T(128)}, s32[]{:T(128)}) while((s32[]{:T(128)}, f32[12,64,128]{2,1,0:T(8,128)S(1)}, s32[]{:T(128)}, f32[8,12,64,128]{3,2,1,0:T(8,128)}, ...), condition=%wide.region_23.24_spmd, body=%wide.region_22.23_spmd.sunk | while | flops 196614 | bytes 1179939 | solution.py:33
  221.3 8.2 %multiply_reduce_fusion.8 = (f32[2,256,12]{1,2,0:T(8,128)S(1)}, f32[2,256,12]{1,2,0:T(8,128)S(1)}, f32[2,256,12,64]{1,3,2,0:T(8,128)}, f32[2,256,12]{1,2,0:T(8,128)S(1)}) fusion(f32[2,256,12,64]{1,3,2,0:T(8,128)S(1)} %fusion.120, f32[2,256,12,64]{1,0,3,2:T(2,128)S(1)} %copy-done.14, f32[2,256,12]{1,2,0:T(8,128)S(1)} %copy-done.48, ...), kind=kOutput, calls=%fused_computation.78 | convolution fusion | flops 1218951168 | bytes 8667184 | tf_op jit(solution)/shard_map/chts,cthp->cshp/dot_general | solution.py:62
  246.0 5.1 scatter-add.25
  254.0 5.0 scatter-add.26
  281.0 5.6 fusion.97
  291.5 119.9 %all-reduce.10.cloned.1.call-done = (f32[512,1536]{1,0:T(8,128)}, f32[512,256]{1,0:T(8,128)}) async-done(((f32[512,1536]{1,0:T(8,128)}, f32[512,256]{1,0:T(8,128)}), (f32[512,1536]{1,0:T(8,128)}, f32[512,256]{1,0:T(8,128)})) %all-reduce.10.cloned.1.call-update) | async-done | bytes 3670032 | tf_op jit(solution)/shard_map/psum | solution.py:309
  429.2 19.3 %reduce-scatter.19.cloned.1.call-done = f32[192,12]{1,0:T(8,128)} async-done(((f32[1536,12]{1,0:T(8,128)}), f32[192,12]{1,0:T(8,128)}) %reduce-scatter.19.cloned.1.call-update) | async-done | bytes 9232
  450.1 37.0 %all-gather.7.cloned.1.call-done = bf16[512,1536]{1,0:T(8,128)(2,1)} async-done(((bf16[128,1536]{1,0:T(8,128)(2,1)}), bf16[512,1536]{1,0:T(8,128)(2,1)}) %all-gather.7.cloned.1.call-update) | async-done | bytes 1572880 | tf_op jit(solution)/shard_map/all_gather | solution.py:216
  492.1 25.0 %all-reduce.6 = (f32[1536]{0:T(1024)S(1)}, f32[4,768]{1,0:T(4,128)}, f32[768]{0:T(1024)}, f32[4,256]{1,0:T(4,128)}, f32[256]{0:T(256)}, /*index=5*/f32[12]{0:T(128)}, f32[12]{0:T(128)}, f32[12]{0:T(128)}, f32[768]{0:T(1024)}) all-reduce(f32[1536]{0:T(1024)S(1)} %get-tuple-element.527, ...), channel_id=6, replica_groups=mesh['dp'=8,'tensor'=4] {'dp'}, use_global_device_ids=true, to_apply=%region_40.41.clone | all-reduce | flops 7460 | bytes 59680
  521.7 22.2 %reduce-scatter.17.cloned.1.call-done = f32[768,192]{0,1:T(8,128)} async-done(((f32[768,1536]{0,1:T(8,128)}), f32[768,192]{0,1:T(8,128)}) %reduce-scatter.17.cloned.1.call-update) | async-done | bytes 589840 | tf_op jit(solution)/shard_map/reduce_scatter | solution.py:318
  543.9 58.3 %reduce-scatter.11.cloned.1.call-done = f32[192,768]{1,0:T(8,128)} async-done(((f32[1536,768]{1,0:T(8,128)}), f32[192,768]{1,0:T(8,128)}) %reduce-scatter.11.cloned.1.call-update) | async-done | bytes 589840 | tf_op jit(solution)/shard_map/reduce_scatter | solution.py:314
  602.2 42.4 %reduce-scatter.15.cloned.1.call-done = f32[192,256]{1,0:T(8,128)} async-done(((f32[1536,256]{1,0:T(8,128)}), f32[192,256]{1,0:T(8,128)}) %reduce-scatter.15.cloned.1.call-update) | async-done | bytes 196624 | tf_op jit(solution)/shard_map/reduce_scatter | solution.py:316
  644.6 57.8 %reduce-scatter.13.cloned.1.call-done = f32[192,768]{1,0:T(8,128)} async-done(((f32[1536,768]{1,0:T(8,128)}), f32[192,768]{1,0:T(8,128)}) %reduce-scatter.13.cloned.1.call-update) | async-done | bytes 589840 | tf_op jit(solution)/shard_map/reduce_scatter | solution.py:315
  (424 shorter events, 206.2 us)
Async XLA Ops:
  7.2 118.3 %copy-start = (bf16[768,1536]{1,0:T(8,128)(2,1)S(1)}, bf16[768,1536]{1,0:T(8,128)(2,1)}, u32[]{:S(2)}) copy-start(bf16[768,1536]{1,0:T(8,128)(2,1)} %param.62) | copy-start | bytes 7077892
  7.2 80.1 %all-gather.9.cloned.1.call-start = ((), (), s32[]{:S(2)}) async-start(), calls=%async_computation.12 | async-start | bytes 3538944 | tf_op jit(solution)/shard_map/all_gather | solution.py:24
  9.8 13.6 %copy-start.76 = (f32[512]{0:T(512)}, f32[512]{0:T(512)S(1)}, u32[]{:S(2)}) copy-start(f32[512]{0:T(512)S(1)} %get-tuple-element.645) | copy-start | bytes 6148
  13.7 10.3 %copy-start.59 = (bf16[1536,12]{0,1:T(8,128)(2,1)S(1)}, bf16[1536,12]{0,1:T(8,128)(2,1)}, u32[]{:S(2)}) copy-start(bf16[1536,12]{0,1:T(8,128)(2,1)} %param.53) | copy-start | bytes 110596
  13.7 23.0 %collective-permute-start = (bf16[3,768]{1,0:T(4,128)(2,1)}, bf16[3,768]{1,0:T(4,128)(2,1)}, u32[]{:S(2)}, u32[]{:S(2)}) collective-permute-start(bf16[3,768]{1,0:T(4,128)(2,1)} %slice.322), channel_id=1, source_target_pairs={{0,4},{4,8},{8,12},{12,16},{16,20},{20,24},{24,28},{1,5},{5,9},{9,... | collective-permute-start | bytes 13832 | tf_op jit(solution)/shard_map/ppermute | solution.py:17
  17.5 16.4 %collective-permute-start.1 = (bf16[3,256]{1,0:T(4,128)(2,1)S(1)}, bf16[3,256]{1,0:T(4,128)(2,1)}, u32[]{:S(2)}, u32[]{:S(2)}) collective-permute-start(bf16[3,256]{1,0:T(4,128)(2,1)S(1)} %slice.329), channel_id=1, source_target_pairs={{0,4},{4,8},{8,12},{12,16},{16,20},{20,24},{24,28},{1,5},{5,9},{9,... | collective-permute-start | bytes 4616 | tf_op jit(solution)/shard_map/ppermute | solution.py:17
  55.0 146.4 %all-gather.11.cloned.1.call-start = ((), (), s32[]{:S(2)}) async-start(), calls=%async_computation.13 | async-start | bytes 3538944 | tf_op jit(solution)/shard_map/all_gather | solution.py:24
  108.7 16.8 %copy-start.90 = (f32[768]{0:T(1024)S(1)}, f32[768]{0:T(1024)}, u32[]{:S(2)}) copy-start(f32[768]{0:T(1024)} %param.61) | copy-start | bytes 9220
  125.5 14.1 %copy-start.86 = (f32[512]{0:T(512)}, f32[512]{0:T(512)S(1)}, u32[]{:S(2)}) copy-start(f32[512]{0:T(512)S(1)} %get-tuple-element.647) | copy-start | bytes 6148
  159.2 119.1 %reduce-scatter.9.cloned.1.call-start = ((), (), s32[]{:S(2)}) async-start(), calls=%async_computation.6 | async-start | bytes 3932160 | tf_op jit(solution)/shard_map/reduce_scatter | solution.py:210
  159.3 13.6 %copy-start.51 = (f32[2,256,12]{1,2,0:T(8,128)S(1)}, f32[2,256,12]{1,2,0:T(8,128)}, u32[]{:S(2)}) copy-start(f32[2,256,12]{1,2,0:T(8,128)} %copy.211) | copy-start | bytes 73732
  185.1 226.4 %all-reduce.10.cloned.1.call-start = ((), (), s32[]{:S(2)}) async-start(), calls=%async_computation.15 | async-start | bytes 7340032 | tf_op jit(solution)/shard_map/psum | solution.py:309
  201.5 14.5 %copy-start.6 = (f32[2,12,64,128]{3,2,1,0:T(8,128)S(1)}, f32[2,12,64,128]{3,2,1,0:T(8,128)}, u32[]{:S(2)}) copy-start(f32[2,12,64,128]{3,2,1,0:T(8,128)} %get-tuple-element.1006) | copy-start | bytes 2359300
  259.8 7.6 %collective-permute-start.2 = (f32[3,768]{1,0:T(4,128)S(1)}, f32[3,768]{1,0:T(4,128)S(1)}, u32[]{:S(2)}, u32[]{:S(2)}) collective-permute-start(f32[3,768]{1,0:T(4,128)S(1)} %slice.342), channel_id=1, source_target_pairs={{4,0},{8,4},{12,8},{16,12},{20,16},{24,20},{28,24},{5,1},{9,5},{13... | collective-permute-start | bytes 27656 | tf_op jit(solution)/shard_map/ppermute | solution.py:17
  273.1 175.4 %reduce-scatter.19.cloned.1.call-start = ((), (), s32[]{:S(2)}) async-start(), calls=%async_computation.14 | async-start | bytes 884736
  278.2 208.8 %all-gather.7.cloned.1.call-start = ((), (), s32[]{:S(2)}) async-start(), calls=%async_computation.7 | async-start | bytes 1966080 | tf_op jit(solution)/shard_map/all_gather | solution.py:216
  280.9 263.0 %reduce-scatter.17.cloned.1.call-start = ((), (), s32[]{:S(2)}) async-start(), calls=%async_computation.11 | async-start | bytes 5308416 | tf_op jit(solution)/shard_map/reduce_scatter | solution.py:318
  286.7 315.5 %reduce-scatter.11.cloned.1.call-start = ((), (), s32[]{:S(2)}) async-start(), calls=%async_computation.8 | async-start | bytes 5308416 | tf_op jit(solution)/shard_map/reduce_scatter | solution.py:314
  291.5 120.0 %copy-start.27 = (f32[512,256]{1,0:T(8,128)S(1)}, f32[512,256]{1,0:T(8,128)}, u32[]{:S(2)}) copy-start(f32[512,256]{1,0:T(8,128)} %get-tuple-element.625) | copy-start | bytes 1572868
  291.5 353.1 %reduce-scatter.15.cloned.1.call-start = ((), (), s32[]{:S(2)}) async-start(), calls=%async_computation.10 | async-start | bytes 1769472 | tf_op jit(solution)/shard_map/reduce_scatter | solution.py:316
  418.1 3.1 collective-permute-start.3
  423.3 279.0 %reduce-scatter.13.cloned.1.call-start = ((), (), s32[]{:S(2)}) async-start(), calls=%async_computation.9 | async-start | bytes 5308416 | tf_op jit(solution)/shard_map/reduce_scatter | solution.py:315
  487.1 30.6 %copy-start.32 = (bf16[512,1536]{1,0:T(8,128)(2,1)S(1)}, bf16[512,1536]{1,0:T(8,128)(2,1)}, u32[]{:S(2)}) copy-start(bf16[512,1536]{1,0:T(8,128)(2,1)} %param.63) | copy-start | bytes 4718596
  487.1 30.6 %copy-start.85 = (f32[512]{0:T(512)S(1)}, f32[512]{0:T(512)}, u32[]{:S(2)}) copy-start(f32[512]{0:T(512)} %get-tuple-element.644) | copy-start | bytes 6148
  (94 other events, 306.7 us)
Sparse Core Ops, SparseCore 0:
  55.1 32.1 all-gather.8
  159.3 42.0 all-gather.10
  203.7 60.2 reduce-scatter.8
  273.2 138.2 all-reduce.9
  414.4 34.0 reduce-scatter.18
  449.9 37.0 all-gather.6
  491.1 52.7 reduce-scatter.16
  548.3 53.8 reduce-scatter.10
  606.0 38.4 reduce-scatter.14
  648.4 53.8 reduce-scatter.12
where the time goes:
time: 721 us; the launch traced here: 712 us
  waiting for transfers between devices  386 us (54%)
  matrix products  98.2 us (14%)
  local copies, waits for them, and re-layouts  82.9 us (11%)
  other arithmetic  58.5 us (8%)
  blocking collectives  57.1 us (8%)
  between operations  17.2 us (2%)
  starting transfers between devices  11.1 us (2%)
    psum x1, waiting for transfers between devices, on_device(): lax.psum(partial_in, 'tensor') + matmul_rt(grad_state_low, state_proj)  120 us
    reduce_scatter x1, waiting for transfers between devices, on_device(): lax.psum_scatter(gate_g, 'dp', scatter_dimension=0, tiled=True)  58.3 us
    reduce_scatter x1, waiting for transfers between devices, on_device(): lax.psum_scatter(value_g, 'dp', scatter_dimension=0, tiled=True)  57.8 us
    dot_general x11, matrix products, exact(): return jnp.einsum(form, left, right, precision=lax.Precision.HIGHEST)  48.3 us
    reduce_scatter x1, waiting for transfers between devices, on_device(): lax.psum_scatter(state_g, 'dp', scatter_dimension=0, tiled=True)  42.4 us
    all_gather x1, waiting for transfers between devices, on_device(): lax.all_gather((own_rows + share_sum).astype(jnp.bfloat16), 'tensor', axi...  37 us
    unnamed x2, blocking collectives  36.9 us
    all_gather x2, waiting for transfers between devices, carried_in(): gathered = jax.tree.map(lambda a: lax.all_gather(a, axis), part)  27.5 us
  transfers between devices with their start and end apart: 14, of which 10 were waited for; matrix products, arithmetic and copies ran while one was open for 22% of the time, Pallas kernels for 0%

commit v1 on v0

v1 whole, which is shorter than its diff:
```python
import functools
import types

import jax
import jax.numpy as jnp
from jax import lax
from jax.experimental import pallas as pl
from jax.experimental.pallas import tpu as pltpu
from jax.sharding import PartitionSpec as P

F32 = jnp.float32
BF = jnp.bfloat16
MAXLEN = 2048
HEADDIM = 64
L = 128
RT = 32
LANES = 128
SUB = 256
HALO = 16
EPS = 1e-05
NEG = -1e30
VMEM_BYTES = 64 * 1024 * 1024 - 4096
DP = "dp"
TP = "tensor"


def mm(a, b):
    return lax.dot_general(a, b, (((1,), (0,)), ((), ())), preferred_element_type=F32)


def mm_rt(a, b):
    return lax.dot_general(a, b, (((1,), (1,)), ((), ())), preferred_element_type=F32)


def mm_lt(a, b):
    return lax.dot_general(a, b, (((0,), (0,)), ((), ())), preferred_element_type=F32)


def parts(a, n):
    out = []
    for _ in range(n - 1):
        hi = a.astype(BF)
        out.append(hi)
        a = a - hi.astype(F32)
    out.append(a.astype(BF))
    return out


def mm_fine(a, b, n=2):
    total = None
    for p in parts(a, n):
        t = mm(p, b)
        total = t if total is None else total + t
    return total


def mm_fine_right(a, b, n=3):
    total = None
    for p in parts(b, n):
        t = mm(a, p)
        total = t if total is None else total + t
    return total


def mm_rt_fine(a, b, n=3):
    total = None
    for p in parts(a, n):
        t = mm_rt(p, b)
        total = t if total is None else total + t
    return total


def wide(a, n):
    return jnp.concatenate([a] * n, axis=1) if n > 1 else a


def fold8(a):
    total = a[0:8]
    for i in range(8, a.shape[0], 8):
        total = total + a[i : i + 8]
    return total


def rows_loop(n, size, fn):
    def step(i, carry):
        fn(pl.multiple_of(i * size, size))
        return carry

    lax.fori_loop(0, n // size, step, 0)


def sigmoid(v):
    return 0.5 * jnp.tanh(0.5 * v) + 0.5


def silu_parts(v):
    sig = sigmoid(v)
    return v * sig, sig * (1.0 + v * (1.0 - sig))


class Plan:
    def __init__(self, mesh, x, lens, gw, sw, stepw, cw):
        self.dp = mesh.shape[DP]
        self.tp = mesh.shape[TP]
        self.tok, self.d = x.shape
        self.w = gw.shape[1]
        self.h = stepw.shape[0]
        self.s2 = sw.shape[1]
        self.ns = self.s2 // 2
        self.taps = cw.shape[0]
        self.nseq = lens.shape[0]
        self.total = self.tok * self.dp
        self.nb = self.tok // L
        self.pairs = self.h // 2
        self.nt = 256 if self.w % 256 == 0 else 128
        self.aligned = self.nseq * MAXLEN == self.total and MAXLEN % self.tok == 0
        self.group = MAXLEN // self.tok
        if self.aligned:
            self.reach = 1
        else:
            self.reach = min(-(-(MAXLEN - 1) // self.tok), self.dp - 1)
        self.srows = self.ns if self.aligned else self.ns + HALO
        self.nbits = self.dp.bit_length() - 1
        self.nc = self.d // LANES
        self.nsub = self.tok // SUB
        self.nch = self.nc * self.nsub
        self.cut = self.w // LANES // 2 * LANES
        self.crow = self.d // self.dp
        bits = list(range(self.nbits))
        self.order_a = bits
        self.order_b = bits[:1] + bits[1:][::-1]


def scratch_of(p):
    tok, d, w, ns, s2, nb, dp, tp = p.tok, p.d, p.w, p.ns, p.s2, p.nb, p.dp, p.tp
    v = lambda *s, t=BF: pltpu.VMEM(s, t)
    dma = lambda *s: pltpu.SemaphoreType.DMA(s)
    return dict(
        x=v(tok, d), gw=v(d, w), vw=v(d, w), sw=v(d, s2), ow=v(w, d), og=v(tok, d),
        in_sem=dma(6), pg=v(1, d, t=F32), cb=v(1, w, t=F32), ng=v(1, w, t=F32),
        swp=v(LANES, d), small=v(8, LANES, t=F32), E=v(LANES, w), ske=v(8, w, t=F32),
        hx=v(HALO, d), nx=v(tok + HALO, d), tb=v(d, tok), invin=v(tok, LANES, t=F32),
        vraw=v(tok + HALO, w), sraw=v(tok + HALO, s2), vgr=v(tok, w), sgr=v(tok, s2),
        val=v(tok, w), st=v(tok, s2), stT=v(s2, tok), gate=v(tok, w),
        sp=v(tok, LANES, t=F32), steps=v(tok, LANES, t=F32),
        cum=v(tok, LANES, t=F32), cumT=v(LANES, tok, t=F32),
        stepe=v(tok, w, t=F32), care=v(tok, w), taile=v(tok, w),
        facr=v(8 * nb, w, t=F32),
        wtd=v(tok, w), tw=v(tok, w), ends=v(nb, ns, w, t=F32), run=v(ns, w, t=F32),
        D=v(max(nb * p.pairs, p.nch), SUB, LANES), mixer=v(tok, w, t=F32), cp=v(tok, w), gn=v(tok, w),
        dn=v(tok + 8, w, t=F32), STb=v(nb, ns, w),
        sc=v(tok, LANES, t=F32),
        invo=v(tok, LANES, t=F32), coefo=v(tok, LANES, t=F32),
        dgate=v(tok, w), sdm=v(tok, w), rc=v(tok, LANES, t=F32),
        colT=v(LANES, L, t=F32), gsc=v(L, L, t=F32), rs=v(L, LANES, t=F32),
        gBC=v(tok, s2, t=F32), gf=v(8 * nb, w, t=F32), gtl=v(ns, w), dsp=v(tok + 8, s2, t=F32),
        dsl=v(tok, s2), dst=v(tok, LANES),
        acc=v(2, 8, w, t=F32), cacc=v(p.taps + 1, 8, max(w, s2), t=F32), pacc=v(8, d, t=F32),
        sacc=v(4, 8, LANES, t=F32),
        halo_sem=dma(6),
        fbuf=v(p.srows, w), fin=v(max(p.reach, 1), p.srows, w), fsem=dma(2, max(p.reach, 1)),
        bin=v(max(p.reach, 1), p.srows, w), bsem=dma(2, max(p.reach, 1)),
        zx=v(2, tp, 2 * nb, LANES, t=F32), zsem=dma(2, 2, tp),
        zs=v(tp, 8, d // 4, t=F32), zssem=dma(2, tp),
        sm=v(p.nbits + 1, 16, w, t=F32), sm_in=v(p.nbits, 16, w, t=F32), smsem=dma(2, p.nbits),
        Pf=v(p.nch, SUB, LANES), ar_a=v(2, p.nch, SUB, LANES), ar_b=v(p.nch, SUB, LANES),
        arsem=dma(2, 6, p.nch),
        w_gate=v(p.crow, w, t=F32), w_value=v(p.crow, w, t=F32), w_out=v(p.crow, w, t=F32), osem=dma(3),
        sq=v(p.crow, s2), sq_in=v(p.crow, s2), sq_x=v(p.crow, s2), sqsem=dma(5),
        g_out=v(dp, p.crow, w), r_out=v(dp - 1, p.crow, w), s_out=dma(2, dp),
        g_ss=v(dp, p.crow, s2 + LANES), g_gate=v(dp, p.crow, w), r_gate=v(dp - 1, p.crow, w), s_gate=dma(2, dp),
        r_va=v(dp - 1, p.crow, p.cut), s_va=dma(2, dp),
        r_vb=v(dp - 1, p.crow, w - p.cut), s_vb=dma(2, dp),
        r_ss=v(dp - 1, p.crow, s2 + LANES), s_ss=dma(2, dp),
    )


def kernel(p, names, few_in, few_out, *refs):
    r = types.SimpleNamespace(**dict(zip(names, refs)))
    by_name = dict(zip(names, refs))
    few_loads = [
        pltpu.make_async_copy(by_name[HBM + k], by_name[k], r.few_sem.at[0, i]) for i, k in enumerate(few_in)
    ]
    few_gives = [
        pltpu.make_async_copy(by_name[k], by_name[HBM + k], r.few_sem.at[1, i]) for i, k in enumerate(few_out)
    ]
    big = (r.x, r.gw, r.vw, r.sw, r.ow, r.og)
    sources = refs[: len(big)]
    tok, d, w, ns, s2, nb, dp, tp, pairs = p.tok, p.d, p.w, p.ns, p.s2, p.nb, p.dp, p.tp, p.pairs
    me = lax.axis_index(DP)
    rank = lax.axis_index(TP)
    first = me * tok
    wl = w // LANES
    inner = w * tp
    nt = p.nt

    def bit(v, b):
        return lax.rem(v // (2**b), 2)

    def remote(src, dst, ssem, rsem, axis, at):
        return pltpu.make_async_remote_copy(
            src_ref=src,
            dst_ref=dst,
            send_sem=ssem,
            recv_sem=rsem,
            device_id={axis: at},
            device_id_type=pl.DeviceIdType.MESH,
        )

    def load(at):
        return pltpu.make_async_copy(sources[at], big[at], r.in_sem.at[at])

    X, GW, VW, SW, OW, OG = range(len(big))
    load(X).start()
    for c in few_loads:
        c.start()
    for at in (VW, SW):
        load(at).start()

    barrier = pltpu.get_barrier_semaphore()
    for off in range(1, tp):
        pl.semaphore_signal(
            barrier, inc=1, device_id={TP: lax.rem(rank + off, tp)}, device_id_type=pl.DeviceIdType.MESH
        )
    for off in range(1, dp):
        pl.semaphore_signal(
            barrier, inc=1, device_id={DP: lax.rem(me + off, dp)}, device_id_type=pl.DeviceIdType.MESH
        )

    ahead = lax.rem(me, p.group)
    behind = p.group - 1 - ahead
    has_prev = ahead > 0 if p.aligned else me > 0
    has_next = behind > 0 if p.aligned else me < dp - 1
    starts = [jnp.int32(0)]
    for k in range(p.nseq - 1):
        starts.append(starts[-1] + r.lens[k])

    def start_of(g):
        at = jnp.zeros_like(g) if getattr(g, "shape", ()) else jnp.int32(0)
        for s in starts[1:]:
            at = jnp.where(g >= s, s, at)
        return at

    def place(t0, rows, width):
        g = first + t0 + lax.broadcasted_iota(jnp.int32, (rows, width), 0)
        return g - start_of(g)

    for c in few_loads:
        c.wait()
    row_w = lax.broadcasted_iota(jnp.int32, (LANES, w), 0)
    lane_w = lax.broadcasted_iota(jnp.int32, (LANES, w), 1)
    r.E[...] = jnp.where(lane_w // HEADDIM == row_w, 1.0, 0.0).astype(BF)
    r.small[...] = jnp.zeros((8, LANES), F32)
    r.small[0:1, 0 : p.h] = r.sb[...]
    r.small[1:2, 0 : p.h] = r.dl[...]
    r.small[2:3, 0 : p.h] = r.sk[...]
    r.ske[...] = mm_fine(jnp.broadcast_to(r.small[2:3, :], (8, LANES)), r.E[...], 3)
    r.swp[...] = jnp.zeros((LANES, d), BF)
    r.swp[0 : p.h, :] = r.stepw[...]
    r.pg[...] = r.pg_in[...].reshape(1, d)
    r.cb[...] = r.cb_in[...].reshape(1, w)
    r.ng[...] = r.ng_in[...].reshape(1, w)
    skip_row = r.ske[0:1, :]
    bias_row = r.small[0:1, :]
    decay_row = -jnp.exp(r.small[1:2, :])
    lane_l = lax.broadcasted_iota(jnp.int32, (L, LANES), 1)
    row_l = lax.broadcasted_iota(jnp.int32, (L, LANES), 0)

    load(X).wait()
    for at in (GW, OG, OW):
        load(at).start()
    pl.semaphore_wait(barrier, tp - 1 + dp - 1)

    def halo_copy():
        return remote(
            r.x.at[pl.ds(tok - HALO, HALO), :], r.hx, r.halo_sem.at[0], r.halo_sem.at[1],
            DP, jnp.minimum(me + 1, dp - 1),
        )

    @pl.when(has_next)
    def _():
        halo_copy().start()

    @pl.when(jnp.logical_not(has_prev))
    def _():
        r.hx[...] = jnp.zeros((HALO, d), BF)

    def ok_fwd(k, at):
        c = at >= k
        return jnp.logical_and(c, lax.rem(at, p.group) >= k) if p.aligned else c

    def ok_bwd(k, at):
        c = at + k < dp
        return jnp.logical_and(c, lax.rem(at, p.group) + k < p.group) if p.aligned else c

    def fwd_copy(k):
        return remote(
            r.fbuf, r.fin.at[k - 1], r.fsem.at[0, k - 1], r.fsem.at[1, k - 1], DP,
            jnp.minimum(me + k, dp - 1),
        )

    def bwd_copy(k):
        return remote(
            r.fbuf, r.bin.at[k - 1], r.bsem.at[0, k - 1], r.bsem.at[1, k - 1], DP,
            jnp.maximum(me - k, 0),
        )

    for k in range(1, p.reach + 1):

        @pl.when(jnp.logical_not(ok_fwd(k, me)))
        def _(k=k):
            r.fin[k - 1] = jnp.zeros((p.srows, w), BF)

        @pl.when(jnp.logical_not(ok_bwd(k, me)))
        def _(k=k):
            r.bin[k - 1] = jnp.zeros((p.srows, w), BF)

    def own_factor():
        f = r.facr[0:1, :]
        for c in range(1, nb):
            f = f * r.facr[8 * c : 8 * c + 1, :]
        return f


    def pass_on(copy, slots, first):
        f = own_factor()

        def body(t):
            rr = pl.ds(t, RT)
            state = r.run[rr, :]
            if not first:
                state = state + f * slots[0, rr, :].astype(F32)
            r.fbuf[rr, :] = state.astype(BF)

        rows_loop(ns, RT, body)
        copy(1).start()

    def send_states(copy, turn, has):
        if p.aligned:

            @pl.when(jnp.logical_and(turn == 0, turn < p.group - 1))
            def _():
                pass_on(copy, None, True)

            return

        def body(t):
            rr = pl.ds(t, RT)
            r.fbuf[rr, :] = r.run[rr, :].astype(BF)

        rows_loop(ns, RT, body)
        r.fbuf[ns : ns + HALO, :] = jnp.broadcast_to(own_factor(), (HALO, w)).astype(BF)
        for k in range(1, p.reach + 1):

            @pl.when(has(k))
            def _(k=k):
                copy(k).start()

    def relay_states(copy, slots, turn, lo, hi):
        if p.aligned:
            hi = min(hi, p.group - 1)
            if lo < hi:

                @pl.when(jnp.logical_and(turn >= lo, turn < hi))
                def _():
                    copy(1).wait_recv()
                    pass_on(copy, slots, False)

    def receive_states(copy, slots, turn, has):
        if p.aligned:

            @pl.when(jnp.logical_and(turn == p.group - 1, turn > 0))
            def _():
                copy(1).wait_recv()

            def body(t):
                rr = pl.ds(t, RT)
                r.run[rr, :] = slots[0, rr, :].astype(F32)

            rows_loop(ns, RT, body)
            return

        for k in range(1, p.reach + 1):

            @pl.when(has(k))
            def _(k=k):
                copy(k).wait_recv()

        def body(t):
            rr = pl.ds(t, RT)
            total = jnp.zeros((RT, w), F32)
            f = jnp.ones((1, w), F32)
            for k in range(p.reach):
                total = total + f * slots[k, rr, :].astype(F32)
                f = f * slots[k, ns : ns + HALO, :].astype(F32)[0:1]
            r.run[rr, :] = total

        rows_loop(ns, RT, body)

    def ar_sems(ph, kind, i):
        return r.arsem.at[ph, kind, i]

    def cols(i):
        return pl.ds(pl.multiple_of(i * LANES, LANES), LANES)

    nsub = p.nsub
    ar_src = (r.Pf, r.D)

    nch = p.nch

    def columns(i):
        return cols(i // nsub)

    def row0(i):
        return pl.multiple_of(lax.rem(i, nsub) * SUB, SUB) if isinstance(i, jax.Array) else i % nsub * SUB

    ar_dst = (r.o_block, r.o_input)

    half_t = tp // 2
    mid = jnp.logical_or(rank == half_t - 1, rank == half_t)
    inward = jnp.where(rank < half_t, rank + 1, rank - 1)
    outward = jnp.clip(jnp.where(rank < half_t, rank - 1, rank + 1), 0, tp - 1)
    end = jnp.logical_or(rank == 0, rank == tp - 1)
    ar_across = (r.ar_b, r.Pf)

    def ar_a(ph, i):
        return r.ar_a.at[ph, i]

    def ar_in(ph, i, src):
        return remote(src, ar_a(ph, i), ar_sems(ph, 0, i), ar_sems(ph, 1, i), TP, inward)

    def ar_swap(ph, i):
        return remote(
            ar_a(ph, i), ar_across[ph].at[i], ar_sems(ph, 0, i), ar_sems(ph, 2, i), TP, inward
        )

    def ar_out(ph, i, src):
        return remote(src, ar_a(ph, i), ar_sems(ph, 3, i), ar_sems(ph, 4, i), TP, outward)

    def ar_keep(ph, i, src):
        return pltpu.make_async_copy(src, ar_dst[ph].at[pl.ds(row0(i), SUB), columns(i)], ar_sems(ph, 5, i))

    def each_rows(i, fn):
        base = row0(i)
        rows_loop(SUB, L, lambda t: fn(pl.ds(t, L), pl.ds(pl.multiple_of(base + t, L), L)))

    def ar_start(ph, i):
        @pl.when(end)
        def _():
            ar_in(ph, i, ar_src[ph].at[i]).start()

    def ar_add(ph, i):
        @pl.when(end)
        def _():
            ar_in(ph, i, ar_a(ph, i)).wait_send()
            to, at = divmod(ph * nch + i + DEPTH, nch)
            if to < 2:
                ar_in(to, at, ar_src[to].at[at]).start()

        @pl.when(jnp.logical_not(end))
        def _():
            ar_in(ph, i, ar_a(ph, i)).wait_recv()

            def body(q, rr):
                r.ar_a[ph, i, q, :] = (r.ar_a[ph, i, q, :].astype(F32) + ar_src[ph][i, q, :].astype(F32)).astype(BF)

            each_rows(i, body)
            if half_t > 2:

                @pl.when(jnp.logical_not(mid))
                def _():
                    ar_in(ph, i, ar_a(ph, i)).start()

            @pl.when(mid)
            def _():
                ar_swap(ph, i).start()

    def ar_done(ph, i):
        @pl.when(mid)
        def _():
            ar_swap(ph, i).wait()
            got = ar_across[ph]

            def body(q, rr):
                total = r.ar_a[ph, i, q, :].astype(F32) + got[i, q, :].astype(F32)
                xt = r.x[rr, columns(i)].astype(F32)
                if ph == 0:
                    res = xt + total * r.invo[rr, :]
                else:
                    f = total * r.pg[0:1, columns(i)]
                    res = r.og[rr, columns(i)].astype(F32) + r.invin[rr, :] * f - xt * r.coefo[rr, :]
                got[i, q, :] = res.astype(BF)

            each_rows(i, body)
            ar_out(ph, i, got.at[i]).start()
            ar_keep(ph, i, got.at[i]).start()

        if half_t > 2:

            @pl.when(jnp.logical_not(jnp.logical_or(mid, end)))
            def _():
                here = ar_a(ph, i)
                ar_in(ph, i, here).wait_send()
                ar_out(ph, i, here).wait_recv()
                ar_out(ph, i, here).start()
                ar_keep(ph, i, here).start()

    def ar_finish(ph, i):
        here = ar_a(ph, i)

        @pl.when(end)
        def _():
            ar_out(ph, i, here).wait_recv()
            ar_keep(ph, i, here).start()

        @pl.when(jnp.logical_not(end))
        def _():
            ar_out(ph, i, here).wait_send()

    def ar_kept(ph, i):
        ar_keep(ph, i, ar_a(ph, i)).wait()

    LAG = 3
    DEPTH = 4
    FIN = LAG + 6
    KEPT = FIN + 4
    last_step = 2 * nch + LAG

    def ar_service(s0, s1):
        for s in range(s0, min(s1, last_step)):
            if s < 2 * nch:
                ar_add(*divmod(s, nch))
            if s >= LAG:
                ar_done(*divmod(s - LAG, nch))
            if s >= FIN:
                ar_finish(*divmod(s - FIN, nch))
            if s >= KEPT:
                ar_kept(*divmod(s - KEPT, nch))

    p_out = (r.g_out, 0, w, r.r_out, r.s_out, p.order_a)
    p_gate = (r.g_gate, 0, w, r.r_gate, r.s_gate, p.order_b)
    p_va = (r.g_out, 0, p.cut, r.r_va, r.s_va, p.order_a)
    p_vb = (r.g_out, p.cut, w, r.r_vb, r.s_vb, p.order_b)
    p_ss = (r.g_ss, 0, s2 + LANES, r.r_ss, r.s_ss, p.order_a)

    def rs_copy(piece, s, idx):
        g, lo, hi, got, sems, order = piece
        base = sum(dp // 2 ** (q + 1) for q in range(s))
        k = jnp.int32(0)
        for q in order[:s]:
            k = k + bit(me, q) * 2**q
        rem = [b for b in range(p.nbits) if b not in order[: s + 1]]
        for n, b in enumerate(rem):
            k = k + ((idx >> n) & 1) * 2**b
        b = order[s]
        mine = bit(me, b)
        keep = k + mine * 2**b
        send = k + (1 - mine) * 2**b
        src = g.at[send] if hi - lo == g.shape[2] else g.at[send, :, pl.ds(lo, hi - lo)]
        copy = remote(
            src, got.at[base + idx], sems.at[0, base + idx], sems.at[1, base + idx],
            DP, me + (1 - 2 * mine) * 2**b,
        )
        return copy, keep, base + idx

    def rs_send(piece, s):
        for idx in range(dp // 2 ** (s + 1)):
            rs_copy(piece, s, idx)[0].start()

    def rs_take(piece, s, out=None):
        g, lo, hi, got = piece[:4]
        last = s == p.nbits - 1
        for idx in range(dp // 2 ** (s + 1)):
            copy, keep, at = rs_copy(piece, s, idx)
            copy.wait_recv()

            def body(t, keep=keep, at=at):
                rr = pl.ds(t, RT)
                total = g[keep, rr, lo:hi].astype(F32) + got[at, rr, :].astype(F32)
                if last:
                    out(rr, total)
                else:
                    g[keep, rr, lo:hi] = total.astype(BF)

            rows_loop(p.crow, RT, body)
        if not last:
            rs_send(piece, s + 1)

    def rs_finish(piece):
        for s in range(p.nbits):
            for idx in range(dp // 2 ** (s + 1)):
                rs_copy(piece, s, idx)[0].wait_send()

    def zx_copy(which, off):
        return remote(
            r.zx.at[which, rank], r.zx.at[which, rank], r.zsem.at[which, 0, off], r.zsem.at[which, 1, off],
            TP, lax.rem(rank + off, tp),
        )

    def zx_send(which, src):
        for c in range(nb):
            turned = src[c * L : (c + 1) * L, :].T
            r.zx[which, rank, c : c + 1, :] = turned[0:1]
            r.zx[which, rank, nb + c : nb + c + 1, :] = turned[1:2]
        for off in range(1, tp):
            zx_copy(which, off).start()

    def zx_take(which, dst):
        for off in range(1, tp):
            zx_copy(which, off).wait_recv()
        total = r.zx[which, 0]
        for k in range(1, tp):
            total = total + r.zx[which, k]
        for c in range(nb):
            first = jnp.broadcast_to(total[c : c + 1], (LANES, L))
            second = jnp.broadcast_to(total[nb + c : nb + c + 1], (LANES, L))
            dst[c * L : (c + 1) * L, :] = jnp.where(row_l == 0, first, second).T

    def sm_copy(s):
        mine = bit(me, s)
        return remote(
            r.sm.at[s], r.sm_in.at[s], r.smsem.at[0, s], r.smsem.at[1, s], DP, me + (1 - 2 * mine) * 2**s
        )

    def sm_take(s):
        sm_copy(s).wait_recv()
        r.sm[s + 1] = r.sm[s] + r.sm_in[s]
        if s + 1 < p.nbits:
            sm_copy(s + 1).start()

    def slot_copy(buf, sems, axis, at, count, off):
        return remote(
            buf.at[at], buf.at[at], sems.at[0, off], sems.at[1, off], axis, lax.rem(at + off, count)
        )

    def norm_rows(src, s0, dst0, rows):
        xf = src[pl.ds(s0, rows), :].astype(F32)
        inv = lax.rsqrt(jnp.mean(xf * xf, axis=1, keepdims=True) + EPS)
        r.nx[pl.ds(dst0, rows), :] = (xf * inv * r.pg[...]).astype(BF)
        return inv

    def body(t):
        inv = norm_rows(r.x, t, pl.multiple_of(t + HALO, HALO), RT)
        r.invin[pl.ds(t, RT), :] = jnp.broadcast_to(inv, (RT, LANES))

    rows_loop(tok, RT, body)

    @pl.when(has_prev)
    def _():
        halo_copy().wait_recv()

    norm_rows(r.hx, 0, 0, HALO)
    load(VW).wait()
    load(SW).wait()

    def body(n):
        nn = pl.ds(n, nt)
        r.vraw[:, nn] = mm(r.nx[...], r.vw[:, nn]).astype(BF)

    rows_loop(w, nt, body)
    r.sraw[...] = mm(r.nx[...], r.sw[...]).astype(BF)
    r.sp[...] = mm_rt(r.nx[HALO : HALO + tok, :], r.swp[...]).astype(BF).astype(F32) + bias_row

    def conv(raw, cw, cb, width, val, grad):
        def body(t):
            win = raw[pl.ds(t, RT + HALO), :].astype(F32)
            at = None if p.aligned else place(t, RT, width)
            total = jnp.broadcast_to(cb[...], (RT, width))
            for k in range(p.taps):
                back = p.taps - 1 - k
                tap = win[HALO - back : HALO - back + RT]
                if back and not p.aligned:
                    tap = jnp.where(at >= back, tap, 0.0)
                total = total + cw[k : k + 1, :] * tap
            act, slope = silu_parts(total)
            val[pl.ds(t, RT), :] = act.astype(BF)
            grad[pl.ds(t, RT), :] = slope.astype(BF)

        rows_loop(tok, RT, body)

    conv(r.sraw, r.scw, r.scb, s2, r.st, r.sgr)
    conv(r.vraw, r.cw, r.cb, w, r.val, r.vgr)

    for c in range(nb):
        r.stT[:, c * L : (c + 1) * L] = r.st[c * L : (c + 1) * L, :].T

    tri = jnp.where(row_l >= lane_l, 1.0, 0.0).astype(BF)
    for c in range(nb):
        rr = slice(c * L, (c + 1) * L)
        b0 = first + c * L
        pre = r.sp[rr, :]
        steps = jnp.maximum(pre, 0.0) + jnp.log1p(jnp.exp(-jnp.abs(pre)))
        cum = mm_fine_right(tri, decay_row * steps, 3)
        r.steps[rr, :] = steps
        r.cum[rr, :] = cum
        r.cumT[:, rr] = cum.T
        car = jnp.exp(cum)
        tail = jnp.exp(cum[L - 1 : L, :] - cum)
        if not p.aligned:
            g = b0 + row_l
            car = jnp.where(start_of(g) < b0, car, 0.0)
            tail = jnp.where(g >= start_of(b0 + L - 1), tail, 0.0)
        r.invo[rr, :] = car
        r.coefo[rr, :] = tail
        last = mm_fine(car[L - 8 : L, :], r.E[...], 2)[7:8]
        r.facr[8 * c : 8 * c + 8, :] = jnp.broadcast_to(last, (8, w))

    def body(n):
        nn = pl.ds(n, nt)
        r.stepe[:, nn] = mm_fine(r.steps[...], r.E[:, nn], 2)
        r.care[:, nn] = mm(r.invo[...].astype(BF), r.E[:, nn]).astype(BF)
        r.taile[:, nn] = mm(r.coefo[...].astype(BF), r.E[:, nn]).astype(BF)

    rows_loop(w, nt, body)

    def body(t):
        rr = pl.ds(t, RT)
        weighted = r.val[rr, :].astype(F32) * r.stepe[rr, :]
        r.wtd[rr, :] = weighted.astype(BF)
        r.tw[rr, :] = (weighted * r.taile[rr, :].astype(F32)).astype(BF)

    rows_loop(tok, RT, body)

    r.run[...] = jnp.zeros((ns, w), F32)
    for c in range(nb):
        rr = slice(c * L, (c + 1) * L)
        r.ends[c] = mm(r.stT[0:ns, rr], r.tw[rr, :])
        f = r.facr[8 * c : 8 * c + 1, :]

        def body(t, c=c, f=f):
            q = pl.ds(t, RT)
            r.run[q, :] = r.ends[c, q, :] + f * r.run[q, :]

        rows_loop(ns, RT, body)
    send_states(fwd_copy, ahead, lambda k: ok_bwd(k, me))

    def in_block(c):
        rr = pl.ds(pl.multiple_of(c * L, L), L)
        b_rows = r.st[rr, 0:ns]
        c_rows = r.st[rr, ns:s2]
        return rr, b_rows, c_rows, mm_rt(c_rows, b_rows)

    def within(c, carry):
        rr, b_rows, c_rows, scores = in_block(c)
        gt = first + c * L + row_l
        gs = first + c * L + lane_l
        keep = gs <= gt
        if not p.aligned:
            keep = jnp.logical_and(keep, gs >= start_of(gt))
        bias = jnp.where(keep, 0.0, NEG)
        cum = r.cum[rr, :]
        cumt = r.cumT[:, rr]
        for pr in range(pairs):
            decays, mixes = [], []
            for h in (2 * pr, 2 * pr + 1):
                dec = jnp.exp(cum[:, h : h + 1] - cumt[h : h + 1, :] + bias)
                dec = dec.astype(BF)
                decays.append(dec)
                mixes.append((dec.astype(F32) * scores).astype(BF))
            r.D[c * pairs + pr] = jnp.concatenate(decays, axis=0)
            both = mm(jnp.concatenate(mixes, axis=0), r.wtd[rr, pr * LANES : (pr + 1) * LANES])
            r.mixer[rr, pr * LANES : (pr + 1) * LANES] = jnp.where(lane_l < HEADDIM, both[0:L], both[L:])
        return carry

    lax.fori_loop(0, 1, within, 0)
    relay_states(fwd_copy, r.fin, ahead, 1, 2)
    lax.fori_loop(1, nb, within, 0)

    load(GW).wait()

    def body(n):
        nn = pl.ds(n, nt)
        r.gate[:, nn] = mm(r.nx[HALO : HALO + tok, :], r.gw[:, nn]).astype(BF)

    rows_loop(w, nt, body)

    load(OG).wait()
    load(OW).wait()

    def body(n):
        nn = pl.ds(n, nt)
        r.dn[0:tok, nn] = mm_rt(r.og[...], r.ow[nn, :])

    rows_loop(w, nt, body)

    relay_states(fwd_copy, r.fin, ahead, 2, p.group)
    receive_states(fwd_copy, r.fin, ahead, lambda k: ok_fwd(k, me))
    for c in range(nb):
        rr = slice(c * L, (c + 1) * L)
        f = r.facr[8 * c : 8 * c + 1, :]

        def body(t, c=c, f=f):
            q = pl.ds(t, RT)
            now = r.run[q, :]
            hi, lo = parts(now, 2)
            r.STb[c, q, :] = hi
            r.gtl[q, :] = lo
            r.run[q, :] = r.ends[c, q, :] + f * now
            r.ends[c, q, :] = now

        rows_loop(ns, RT, body)
        proj = mm(r.st[rr, ns:s2], r.STb[c]) + mm(r.st[rr, ns:s2], r.gtl[...])
        proj = proj * r.care[rr, :].astype(F32)
        r.cp[rr, :] = proj.astype(BF)
        r.mixer[rr, :] = r.mixer[rr, :] + proj

    lane_t = lax.broadcasted_iota(jnp.int32, (RT, LANES), 1)

    def body(t):
        rr = pl.ds(t, RT)
        mixer = r.mixer[rr, :] + skip_row * r.val[rr, :].astype(F32)
        gate = r.gate[rr, :].astype(F32)
        gated = mixer * (gate * sigmoid(gate))
        gained = gated * r.ng[...]
        r.mixer[rr, :] = mixer
        r.gn[rr, :] = gained.astype(BF)
        squares = jnp.sum(gated * gated, axis=1, keepdims=True)
        cross = jnp.sum(r.dn[rr, :] * gained, axis=1, keepdims=True)
        r.sc[rr, :] = jnp.where(lane_t == 0, squares, jnp.where(lane_t == 1, cross, 0.0))

    rows_loop(tok, RT, body)
    zx_send(0, r.sc)

    def out_tile(n):
        nn = pl.ds(n, 256)
        full = mm(r.gn[...], r.ow[:, nn]).astype(BF)
        for half in range(2):
            for j in range(nsub):
                at = (n // LANES + half) * nsub + j
                r.Pf[at] = full[j * SUB : (j + 1) * SUB, half * LANES : (half + 1) * LANES]

    per_tile = 2 * nsub
    lead = -(-DEPTH // per_tile)
    for n in range(lead):
        out_tile(n * 256)
        for i in range(n * per_tile, min((n + 1) * per_tile, DEPTH)):
            ar_start(0, i)
    rows_loop(d - lead * 256, 256, lambda n: out_tile(pl.multiple_of(n + lead * 256, 256)))

    for c in range(nb):
        r.tb[:, c * L : (c + 1) * L] = r.og[c * L : (c + 1) * L, :].T

    zx_take(0, r.sc)

    def body(t):
        rr = pl.ds(t, L)
        inv = lax.rsqrt(r.sc[rr, 0:1] * (1.0 / inner) + EPS)
        r.invo[rr, :] = jnp.broadcast_to(inv, (L, LANES))
        r.coefo[rr, :] = jnp.broadcast_to(inv * inv * inv * r.sc[rr, 1:2] * (1.0 / inner), (L, LANES))

    rows_loop(tok, L, body)

    r.acc[...] = jnp.zeros((2, 8, w), F32)

    def body(t):
        rr = pl.ds(t, RT)
        mixer = r.mixer[rr, :]
        act, slope = silu_parts(r.gate[rr, :].astype(F32))
        gated = mixer * act
        inv = wide(r.invo[rr, :], wl)
        coef = wide(r.coefo[rr, :], wl)
        dn = r.dn[rr, :]
        scaled = gated * inv
        dgated = inv * (dn * r.ng[...]) - gated * coef
        dmix = dgated * act
        val = r.val[rr, :].astype(F32)
        r.dgate[rr, :] = (dgated * mixer * slope).astype(BF)
        r.gn[rr, :] = (scaled * r.ng[...]).astype(BF)
        r.gate[rr, :] = dmix.astype(BF)
        r.dn[rr, :] = dmix
        hi, lo = parts(dmix * r.care[rr, :].astype(F32), 2)
        r.sdm[rr, :] = hi
        r.care[rr, :] = lo
        r.cp[rr, :] = (dmix * r.cp[rr, :].astype(F32)).astype(BF)
        r.acc[0] = r.acc[0] + fold8(dn * scaled)
        r.acc[1] = r.acc[1] + fold8(dmix * val)

    rows_loop(tok, RT, body)

    r.run[...] = jnp.zeros((ns, w), F32)
    for c in range(nb - 1, -1, -1):
        rr = slice(c * L, (c + 1) * L)
        r.mixer[rr, :] = mm(r.stT[ns:s2, rr], r.sdm[rr, :]) + mm(r.stT[ns:s2, rr], r.care[rr, :])
        f = r.facr[8 * c : 8 * c + 1, :]

        def body(t, c=c, f=f):
            q = pl.ds(t, RT)
            r.run[q, :] = r.mixer[pl.ds(pl.multiple_of(c * L + t, RT), RT), :] + f * r.run[q, :]

        rows_loop(ns, RT, body)
    for k in range(1, p.reach + 1):

        @pl.when(ok_bwd(k, me))
        def _(k=k):
            fwd_copy(k).wait_send()

    send_states(bwd_copy, behind, lambda k: ok_fwd(k, me))

    for c in range(nb):
        rr = slice(c * L, (c + 1) * L)
        r.gtl[...] = (r.ends[c] - r.STb[c].astype(F32)).astype(BF)
        r.gBC[rr, ns:s2] = (
            mm_rt(r.sdm[rr, :], r.STb[c])
            + mm_rt(r.care[rr, :], r.STb[c])
            + mm_rt(r.sdm[rr, :], r.gtl[...])
        )
    r.rc[...] = mm_rt(r.cp[...], r.E[...])
    relay_states(bwd_copy, r.bin, behind, 1, 2)
    ar_service(0, 4)

    def weight_grad(lhs, rhs, into, width, step):
        def body(n):
            nn = pl.ds(n, step)
            full = mm(lhs[...], rhs[:, nn]).astype(BF)
            for k in range(dp):
                into[k, :, nn] = full[k * p.crow : (k + 1) * p.crow, :]

        rows_loop(width, step, body)

    weight_grad(r.tb, r.gn, r.g_out, w, nt)
    rs_send(p_out, 0)
    ar_service(4, 5)

    def transpose_nx():
        for c in range(nb):
            r.tb[:, c * L : (c + 1) * L] = r.nx[HALO + c * L : HALO + (c + 1) * L, :].T

    transpose_nx()
    weight_grad(r.tb, r.dgate, r.g_gate, w, nt)
    rs_send(p_gate, 0)
    ar_service(5, 7)
    rs_take(p_out, 0)

    def within_back(c, carry):
        rr, b_rows, c_rows, scores = in_block(c)
        two = jnp.concatenate([scores, scores], axis=0)
        r.gsc[...] = jnp.zeros((L, L), F32)
        r.rs[...] = r.rc[rr, :]
        r.colT[...] = jnp.zeros((LANES, L), F32)
        low = lane_l < HEADDIM
        for pr in range(pairs):
            pc = slice(pr * LANES, (pr + 1) * LANES)
            dm = r.gate[rr, pc]
            zero = jnp.zeros_like(dm)
            stacked = jnp.concatenate([jnp.where(low, dm, zero), jnp.where(low, zero, dm)], axis=0)
            fine = r.dn[rr, pc] - dm.astype(F32)
            fine = jnp.concatenate([jnp.where(low, fine, 0.0), jnp.where(low, 0.0, fine)], axis=0).astype(BF)
            gm = mm_rt(stacked, r.wtd[rr, pc]) + mm_rt(fine, r.wtd[rr, pc])
            dec = r.D[c * pairs + pr].astype(F32)
            xx = gm * dec
            r.gsc[...] = r.gsc[...] + (xx[0:L] + xx[L:])
            mix = (dec * two).astype(BF)
            gap = (xx * two).astype(BF)
            gapf = gap.astype(F32)
            total = r.rs[...]
            for half in (0, 1):
                h = 2 * pr + half
                hot = jnp.where(lane_l == h, 1.0, 0.0).astype(BF)
                total = total + mm(gap[half * L : (half + 1) * L], hot)
                r.colT[h : h + 1, :] = jnp.sum(gapf[half * L : (half + 1) * L], axis=0, keepdims=True)
            r.rs[...] = total
            r.dn[rr, pc] = mm_lt(mix, stacked)
        low_scores = r.gsc[...].astype(BF)
        r.gBC[rr, ns:s2] = r.gBC[rr, ns:s2] + mm(low_scores, b_rows)
        r.gBC[rr, 0:ns] = mm_lt(low_scores, c_rows)
        r.rc[rr, :] = r.rs[...] - r.colT[...].T
        return carry

    lax.fori_loop(0, nb // 2, within_back, 0)
    rs_take(p_gate, 0)
    ar_service(7, 8)
    lax.fori_loop(nb // 2, nb, within_back, 0)
    ar_service(8, 10)

    relay_states(bwd_copy, r.bin, behind, 2, p.group)
    receive_states(bwd_copy, r.bin, behind, lambda k: ok_bwd(k, me))
    for c in range(nb - 1, -1, -1):
        rr = slice(c * L, (c + 1) * L)
        f = r.facr[8 * c : 8 * c + 1, :]
        r.gf[8 * c : 8 * c + 8, :] = jnp.zeros((8, w), F32)

        def body(t, c=c, f=f):
            q = pl.ds(t, RT)
            now = r.run[q, :]
            gf = r.gf[8 * c : 8 * c + 8, :]
            r.gf[8 * c : 8 * c + 8, :] = gf + fold8(now * r.ends[c, q, :])
            hi, lo = parts(now, 2)
            r.gtl[q, :] = lo
            r.STb[c, q, :] = hi
            r.run[q, :] = r.mixer[pl.ds(pl.multiple_of(c * L + t, RT), RT), :] + f * now

        rows_loop(ns, RT, body)
        gf = jnp.sum(r.gf[8 * c : 8 * c + 8, :], axis=0, keepdims=True) * f
        r.gf[8 * c : 8 * c + 8, :] = jnp.broadcast_to(gf, (8, w))
        r.mixer[rr, :] = mm(r.st[rr, 0:ns], r.STb[c])
        r.gBC[rr, 0:ns] = r.gBC[rr, 0:ns] + (
            mm_rt(r.tw[rr, :], r.STb[c]) + mm_rt(r.tw[rr, :], r.gtl[...])
        )

    def body(t):
        rr = pl.ds(t, RT)
        thr = r.mixer[rr, :]
        gw_ = r.dn[rr, :] + r.taile[rr, :].astype(F32) * thr
        val = r.val[rr, :].astype(F32)
        dval = skip_row * r.gate[rr, :].astype(F32) + gw_ * r.stepe[rr, :]
        r.sdm[rr, :] = (gw_ * val).astype(BF)
        r.cp[rr, :] = (r.tw[rr, :].astype(F32) * thr).astype(BF)
        r.dn[rr, :] = dval * r.vgr[rr, :].astype(F32)
        r.dsp[rr, :] = r.gBC[rr, :] * r.sgr[rr, :].astype(F32)

    rows_loop(tok, RT, body)

    def back_copy(which):
        buf = r.dn if which == 0 else r.dsp
        return remote(
            buf.at[pl.ds(0, 8), :], buf.at[pl.ds(tok, 8), :], r.halo_sem.at[2 + which], r.halo_sem.at[4 + which],
            DP, jnp.maximum(me - 1, 0),
        )

    @pl.when(has_prev)
    def _():
        back_copy(0).start()
        back_copy(1).start()

    @pl.when(jnp.logical_not(has_next))
    def _():
        r.dn[tok : tok + 8, :] = jnp.zeros((8, w), F32)
        r.dsp[tok : tok + 8, :] = jnp.zeros((8, s2), F32)

    ar_service(10, 12)

    up = jnp.where(lane_l >= row_l, 1.0, 0.0).astype(BF)
    below = jnp.where(lane_l < row_l, 1.0, 0.0).astype(BF)
    r.sacc[...] = jnp.zeros((4, 8, LANES), F32)
    for c in range(nb):
        rr = slice(c * L, (c + 1) * L)
        direct = mm_rt(r.sdm[rr, :], r.E[...])
        tails = mm_rt(r.cp[rr, :], r.E[...])
        gf = mm_rt_fine(r.gf[8 * c : 8 * c + 8, :], r.E[...], 3)[0:1]
        q = mm_fine_right(up, r.rc[rr, :], 3) + mm_fine_right(below, tails, 3) + gf
        steps = r.steps[rr, :]
        dstep = decay_row * q + direct
        dpre = dstep * sigmoid(r.sp[rr, :])
        r.dst[rr, :] = dpre.astype(BF)
        r.sacc[0] = r.sacc[0] + fold8(dpre)
        r.sacc[1] = r.sacc[1] + fold8(q * steps * decay_row)


    @pl.when(has_next)
    def _():
        back_copy(0).wait_recv()
        back_copy(1).wait_recv()

    def unmasked(grads, at, back):
        return jnp.where(at >= back, grads, 0.0) if back and not p.aligned else grads

    def conv_back(dpre, cw, width, out, fine=None):
        def body(t):
            grads = dpre[pl.ds(t, RT + 8), :]
            at = None if p.aligned else place(t, RT + 8, width)
            total = jnp.zeros((RT, width), F32)
            for k in range(p.taps):
                back = p.taps - 1 - k
                total = total + cw[k : k + 1, :] * unmasked(grads, at, back)[back : back + RT]
            hi, lo = parts(total, 2)
            out[pl.ds(t, RT), :] = hi
            if fine is not None:
                fine[pl.ds(t, RT), :] = lo

        rows_loop(tok, RT, body)

    conv_back(r.dsp, r.scw, s2, r.st, r.dsl)
    conv_back(r.dn, r.cw, w, r.wtd)


    def keep_out(rr, total):
        r.w_out[rr, :] = total

    def keep_gate(rr, total):
        r.w_gate[rr, :] = total

    def keep_va(rr, total):
        r.w_value[rr, 0 : p.cut] = total

    def keep_vb(rr, total):
        r.w_value[rr, p.cut : w] = total

    def keep_ss(rr, total):
        r.sq[rr, :] = total[:, 0:s2].astype(BF)
        r.sc[rr, :] = total[:, s2 : s2 + LANES]

    ar_service(12, 15)
    rs_take(p_out, 1, keep_out)
    r.pacc[...] = jnp.zeros((8, d), F32)
    r.sc[...] = jnp.zeros((tok, LANES), F32)

    def in_tile(n):
        nn = pl.ds(n, 256)
        r.mixer[:, 0:256] = (
            mm_rt(r.dgate[...], r.gw[nn, :])
            + mm_rt(r.wtd[...], r.vw[nn, :])
            + mm_rt(r.st[...], r.sw[nn, :])
            + mm(r.dst[...], r.swp[:, nn])
        )

        def body(t, j):
            rr = pl.ds(pl.multiple_of(j * SUB + t, RT), RT)
            grad = r.mixer[rr, 0:256]
            gx = grad * r.x[rr, nn].astype(F32)
            r.pacc[:, nn] = r.pacc[:, nn] + fold8(gx * wide(r.invin[rr, :], 2))
            gx = gx * r.pg[0:1, nn]
            r.sc[rr, :] = r.sc[rr, :] + (gx[:, 0:LANES] + gx[:, LANES:])
            low_grad = grad.astype(BF)
            for half in range(2):
                r.D[(n // LANES + half) * nsub + j, pl.ds(t, RT), :] = low_grad[:, half * LANES : (half + 1) * LANES]

        for j in range(nsub):
            rows_loop(SUB, RT, functools.partial(body, j=j))

    rows_loop(d // 2, 256, in_tile)
    ar_service(15, 16)
    rows_loop(d // 2, 256, lambda n: in_tile(pl.multiple_of(n + d // 2, 256)))

    def body(t):
        rr = pl.ds(t, L)
        r.sc[rr, :] = jnp.broadcast_to(jnp.sum(r.sc[rr, :], axis=1, keepdims=True), (L, LANES))

    rows_loop(tok, L, body)
    zx_send(1, r.sc)
    ar_service(16, 19)

    zs, sm = r.zs, r.sm.at[0]
    quarter = d // 4
    sm[...] = jnp.zeros((16, w), F32)

    def conv_sums(raw, dpre, width):
        cacc = r.cacc
        cacc[:, :, 0:width] = jnp.zeros((p.taps + 1, 8, width), F32)

        def body(t):
            win = raw[pl.ds(t, RT + HALO), :].astype(F32)
            grads = dpre[pl.ds(t, RT), :]
            at = None if p.aligned else place(t, RT, width)
            cacc[p.taps, :, 0:width] = cacc[p.taps, :, 0:width] + fold8(grads)
            for k in range(p.taps):
                back = p.taps - 1 - k
                term = unmasked(grads, at, back) * win[HALO - back : HALO - back + RT]
                cacc[k, :, 0:width] = cacc[k, :, 0:width] + fold8(term)

        rows_loop(tok, RT, body)
        return [jnp.sum(cacc[k, :, 0:width], axis=0, keepdims=True) for k in range(p.taps + 1)]

    sums = conv_sums(r.sraw, r.dsp, s2)
    for k in range(p.taps):
        zs[rank, 4 + k : 5 + k, 0:s2] = sums[k]
    for k in range(2):
        zs[rank, 4 + k : 5 + k, s2 : s2 + LANES] = sums[p.taps][:, k * LANES : (k + 1) * LANES]
    zs[rank, 6:8, s2 : s2 + LANES] = jnp.zeros((2, LANES), F32)
    gains = jnp.sum(r.pacc[...], axis=0, keepdims=True)
    for k in range(4):
        zs[rank, k : k + 1, :] = gains[:, k * quarter : (k + 1) * quarter]
    for off in range(1, tp):
        slot_copy(r.zs, r.zssem, TP, rank, tp, off).start()

    ar_service(19, 20)
    zx_take(1, r.sc)

    def body(t):
        rr = pl.ds(t, L)
        inv = r.invin[rr, :]
        r.coefo[rr, :] = inv * inv * inv * (r.sc[rr, 0:1] * (1.0 / d))

    rows_loop(tok, L, body)
    ar_service(20, 21)
    give = [
        pltpu.make_async_copy(src, dst, r.osem.at[i])
        for i, (src, dst) in enumerate(((r.w_out, r.o_out), (r.w_gate, r.o_gate), (r.w_value, r.o_value)))
    ]
    for s in range(2, p.nbits):
        rs_take(p_out, s, keep_out)
    give[0].start()
    ar_service(21, 23)
    rs_take(p_gate, 1, keep_gate)
    rs_finish(p_out)
    weight_grad(r.tb, r.wtd, r.g_out, w, nt)
    rs_send(p_va, 0)
    rs_send(p_vb, 0)
    ar_service(23, 25)
    full = (mm(r.tb[...], r.st[...]) + mm(r.tb[...], r.dsl[...])).astype(BF)
    for k in range(dp):
        r.g_ss[k, :, 0:s2] = full[k * p.crow : (k + 1) * p.crow, :]
    full = mm(r.tb[...], r.dst[...]).astype(BF)
    for k in range(dp):
        r.g_ss[k, :, s2 : s2 + LANES] = full[k * p.crow : (k + 1) * p.crow, :]
    rs_send(p_ss, 0)

    for off in range(1, tp):
        slot_copy(r.zs, r.zssem, TP, rank, tp, off).wait_recv()
    total = zs[0]
    for k in range(1, tp):
        total = total + zs[k]
    sm[8:16, 0:quarter] = total
    sums = conv_sums(r.vraw, r.dn, w)
    for k in range(p.taps + 1):
        sm[k : k + 1, :] = sums[k]
    sm[5:6, :] = jnp.sum(r.acc[0], axis=0, keepdims=True)
    sm[6:7, 0:LANES] = jnp.sum(r.sacc[0], axis=0, keepdims=True)
    sm[6:7, LANES : 2 * LANES] = jnp.sum(r.sacc[1], axis=0, keepdims=True)
    sm[7:8, 0:LANES] = mm_rt_fine(
        jnp.broadcast_to(jnp.sum(r.acc[1], axis=0, keepdims=True), (8, w)), r.E[...], 3
    )[0:1]
    sm_copy(0).start()

    ar_service(25, 27)
    late = ((p_va, keep_va), (p_vb, keep_vb), (p_ss, keep_ss))
    sm_take(0)
    for piece, out in late:
        rs_take(piece, 0, out)
    ar_service(27, 31)
    for s in range(2, p.nbits):
        rs_take(p_gate, s, keep_gate)
    give[1].start()
    ar_service(31, 38)
    at = 38
    for s in range(1, p.nbits):
        sm_take(s)
        for piece, out in late:
            rs_take(piece, s, out)
        if s < p.nbits - 1:
            ar_service(at, at + 7)
            at += 7
    give[2].start()

    def sq_copy(src, dst, ssem, rsem, to):
        return remote(src, dst, r.sqsem.at[ssem], r.sqsem.at[rsem], TP, to)

    sq_in = lambda src: sq_copy(src, r.sq_in, 0, 1, inward)
    sq_swap = lambda: sq_copy(r.sq_in, r.sq_x, 0, 2, inward)
    sq_out = lambda: sq_copy(r.sq_x, r.sq_x, 3, 4, outward)

    def sq_rows(fn):
        rows_loop(p.crow, RT, lambda t: fn(pl.ds(t, RT)))

    @pl.when(end)
    def _():
        sq_in(r.sq).start()

    ar_service(at, at + 2)

    @pl.when(jnp.logical_not(end))
    def _():
        sq_in(r.sq).wait_recv()

        def body(rr):
            r.sq_in[rr, :] = (r.sq_in[rr, :].astype(F32) + r.sq[rr, :].astype(F32)).astype(BF)

        sq_rows(body)
        if half_t > 2:

            @pl.when(jnp.logical_not(mid))
            def _():
                sq_in(r.sq_in).start()

        @pl.when(mid)
        def _():
            sq_swap().start()

    ar_service(at + 2, at + 4)
    at += 4

    @pl.when(mid)
    def _():
        sq_swap().wait()

        def body(rr):
            r.sq_x[rr, :] = (r.sq_in[rr, :].astype(F32) + r.sq_x[rr, :].astype(F32)).astype(BF)

        sq_rows(body)
        sq_out().start()


    for c in range(-(-p.crow // LANES)):
        width = min(LANES, p.crow - c * LANES)
        r.o_step[:, c * LANES : c * LANES + width] = r.sc[c * LANES : (c + 1) * LANES, :].T[0 : p.h, 0:width]

    total = r.sm[p.nbits]
    r.o_cw[...] = total[0 : p.taps]
    r.o_cb[...] = total[p.taps : p.taps + 1]
    r.o_ng[...] = total[5:6]
    r.o_sb[...] = total[6:7, 0 : p.h]
    r.o_dl[...] = total[6:7, LANES : LANES + p.h]
    r.o_sk[...] = total[7:8, 0 : p.h]
    r.o_scw[...] = total[12 : 12 + p.taps, 0:s2]
    for k in range(2):
        r.o_scb[:, k * LANES : (k + 1) * LANES] = total[12 + k : 13 + k, s2 : s2 + LANES]
    own = jnp.zeros((1, p.crow), F32)
    per = quarter // p.crow
    for k in range(dp):
        piece = total[8 + k // per : 9 + k // per, k % per * p.crow : (k % per + 1) * p.crow]
        own = own + jnp.where(me == k, piece, 0.0)
    r.o_pg[...] = own

    for c in few_gives[1:]:
        c.start()
    ar_service(at, last_step)

    @pl.when(jnp.logical_not(mid))
    def _():
        sq_in(r.sq).wait_send()
        sq_out().wait_recv()
        if half_t > 2:

            @pl.when(jnp.logical_not(end))
            def _():
                sq_out().start()

    @pl.when(jnp.logical_not(end))
    def _():
        sq_out().wait_send()

    def body(rr):
        r.o_state[rr, :] = r.sq_x[rr, :].astype(F32)

    sq_rows(body)
    few_gives[0].start()

    for s in range(last_step - FIN, 2 * nch):
        ar_finish(*divmod(s, nch))
    for s in range(last_step - KEPT, 2 * nch):
        ar_kept(*divmod(s, nch))
    for c in give + few_gives:
        c.wait()
    for piece in (p_gate, p_va, p_vb, p_ss):
        rs_finish(piece)
    for off in range(1, tp):
        zx_copy(0, off).wait_send()
        zx_copy(1, off).wait_send()
        slot_copy(r.zs, r.zssem, TP, rank, tp, off).wait_send()
    for s in range(p.nbits):
        sm_copy(s).wait_send()

    @pl.when(has_next)
    def _():
        halo_copy().wait_send()

    @pl.when(has_prev)
    def _():
        back_copy(0).wait_send()
        back_copy(1).wait_send()

    for k in range(1, p.reach + 1):

        @pl.when(ok_fwd(k, me))
        def _(k=k):
            bwd_copy(k).wait_send()


def on_device(
    mesh, x, lens, pg, gw, vw, sw, stepw, cw, cb, scw, scb, sb, dl, sk, ng, ow, og
):
    row = lambda a: a.reshape(1, -1)
    big = (x, gw, vw, sw, ow, og)
    small = dict(
        pg_in=pg, stepw=stepw.T, cw=cw, cb_in=cb, scw=scw, scb=row(scb), sb=row(sb), dl=row(dl),
        sk=row(sk), ng_in=ng,
    )
    p = Plan(mesh, x, lens, gw, sw, stepw.T, cw)
    scratch = scratch_of(p)
    for k, v in small.items():
        scratch[k] = pltpu.VMEM(v.shape, v.dtype)
    f = lambda *s: jax.ShapeDtypeStruct(s, F32)
    rows = jax.ShapeDtypeStruct((p.tok, p.d), BF)
    shapes = dict(
        o_block=rows, o_input=rows, o_pg=f(1, p.crow), o_gate=f(p.crow, p.w), o_value=f(p.crow, p.w),
        o_state=f(p.crow, p.s2), o_step=f(p.h, p.crow), o_cw=f(p.taps, p.w), o_cb=f(1, p.w),
        o_scw=f(p.taps, p.s2), o_scb=f(1, p.s2), o_sb=f(1, p.h), o_dl=f(1, p.h), o_sk=f(1, p.h),
        o_ng=f(1, p.w), o_out=f(p.crow, p.w),
    )
    few_out = tuple(reversed([k for k in shapes if k not in BY_COPY and k != STATE_OUT])) + (STATE_OUT,)
    few_out = few_out[::-1]
    for k in few_out:
        scratch[k] = pltpu.VMEM(shapes[k].shape, F32)
    scratch[FEW_SEM] = pltpu.SemaphoreType.DMA((2, max(len(small), len(few_out))))
    any_ = pl.BlockSpec(memory_space=pl.ANY)
    smem = pl.BlockSpec(memory_space=pltpu.SMEM)
    unnamed = tuple("s" + str(i) for i in range(len(big)))
    hbm = lambda keys: tuple(HBM + k if k in scratch else k for k in keys)
    names = unnamed + ("lens",) + hbm(small) + hbm(shapes) + tuple(scratch)
    outs = pl.pallas_call(
        functools.partial(kernel, p, names, tuple(small), few_out),
        out_shape=tuple(shapes.values()),
        in_specs=[any_] * len(big) + [smem] + [any_] * len(small),
        out_specs=[any_] * len(shapes),
        scratch_shapes=list(scratch.values()),
        compiler_params=pltpu.CompilerParams(
            collective_id=0, has_side_effects=True, vmem_limit_bytes=VMEM_BYTES
        ),
    )(*big, lens, *small.values())
    outs = deliver(outs)
    names = list(shapes)
    turned = (names.index(STEP_OUT), names.index(OUT_OUT))
    return tuple(o.T if i in turned else o for i, o in enumerate(outs))


STEP_OUT, OUT_OUT, STATE_OUT = "o_step", "o_out", "o_state"
HBM, FEW_SEM = "hbm_", "few_sem"
BY_COPY = ("o_block", "o_input", "o_gate", "o_value", "o_out")


def deliver(outs):
    count = len(outs)
    flat = [o.shape[0] == 1 for o in outs]
    shapes = [jax.ShapeDtypeStruct(o.shape[1:] if f else o.shape, o.dtype) for o, f in zip(outs, flat)]

    def body(*refs):
        ins, res, sems = refs[:count], refs[count : 2 * count], refs[2 * count]
        here = refs[2 * count + 1 : 3 * count + 1]
        rows = dict(zip([i for i in range(count) if flat[i]], refs[3 * count + 1 :]))
        reads = [pltpu.make_async_copy(ins[i], here[i], sems.at[0, i]) for i in range(count)]
        writes = [pltpu.make_async_copy(rows.get(i, here[i]), res[i], sems.at[1, i]) for i in range(count)]
        for c in reads:
            c.start()
        for i in range(count):
            reads[i].wait()
            if flat[i]:
                rows[i][...] = here[i][...].reshape(rows[i].shape)
            writes[i].start()
        for c in writes:
            c.wait()

    any_ = pl.BlockSpec(memory_space=pl.ANY)
    return pl.pallas_call(
        body,
        out_shape=shapes,
        in_specs=[any_] * count,
        out_specs=[any_] * count,
        scratch_shapes=[pltpu.SemaphoreType.DMA((2, count))]
        + [pltpu.VMEM(o.shape, o.dtype) for o in outs]
        + [pltpu.VMEM(s.shape, s.dtype) for s, f in zip(shapes, flat) if f],
        compiler_params=pltpu.CompilerParams(vmem_limit_bytes=VMEM_BYTES),
    )(*outs)


def solution(mesh):
    t = TP
    in_specs = (
        P(DP, None), P(), P(), P(None, t), P(None, t), P(), P(None, t), P(None, t), P(t), P(), P(),
        P(t), P(t), P(t), P(t), P(t, None), P(DP, None),
    )
    out_specs = (
        P(DP, None), P(DP, None), P(DP), P(DP, t), P(DP, t), P(DP, None), P(DP, t),
        P(None, t), P(t), P(), P(), P(t), P(t), P(t), P(t), P(t, DP),
    )
    return jax.shard_map(
        functools.partial(on_device, mesh), mesh=mesh, in_specs=in_specs, out_specs=out_specs, check_vma=False
    )
```

time: 721 us -> 132 us (0.18); the launches traced: 712 us -> 132 us
  waiting for transfers between devices: 386 us -> 0 us
  Pallas kernels: 0 us -> 131 us
  matrix products: 98.2 us -> 0 us
  local copies, waits for them, and re-layouts: 82.9 us -> 0 us
  other arithmetic: 58.5 us -> 0 us
  blocking collectives: 57.1 us -> 0 us
  between operations: 17.2 us -> 0.82 us
  starting transfers between devices: 11.1 us -> 0 us
    reduce_scatter x5 -> x0, waiting for transfers between devices: 181 us -> none  [the longest x1 58.3 us: on_device(): lax.psum_scatter(gate_g, 'dp', scatter_dimension=0, tiled=True)]
    pallas_call x0 -> x2, Pallas kernels: none -> 131 us  [the longest x1 127 us: on_device(): pl.pallas_call(functools.partial(kernel, p, names, tuple(small), few_out)...]
    psum x1 -> x0, waiting for transfers between devices: 120 us -> none  [on_device(): lax.psum(partial_in, 'tensor') + matmul_rt(grad_state_low, state_proj)]
    dot_general x26 -> x0, matrix products: 96.5 us -> none  [the longest x11 48.3 us: exact(): return jnp.einsum(form, left, right, precision=lax.Precision.HIGHEST)]
    all_gather x3 -> x0, waiting for transfers between devices: 64.5 us -> none  [the longest x1 37 us: on_device(): lax.all_gather((own_rows + share_sum).astype(jnp.bfloat16), 'tensor', axi...]
    unnamed x2 -> x0, blocking collectives: 36.9 us -> none
    psum x2 -> x0, blocking collectives: 20.2 us -> none  [the longest x1 11.7 us: on_device(): lax.psum(jnp.sum(gated_out * gated_out, axis=1), 'tensor')]
    unnamed x11 -> x0, waiting for transfers between devices: 19.5 us -> none
  transfers between devices with their start and end apart: 14 -> 0, of which waited for: 10 -> 0; matrix products, arithmetic and copies ran while one was open for 22% -> 0% of each run, Pallas kernels for 0% -> 0%
where the time goes in v1:
time: 132 us
  Pallas kernels  131 us (99%)
    pallas_call x1, Pallas kernels, on_device(): pl.pallas_call(functools.partial(kernel, p, names, tuple(small), few_out)...  127 us
    pallas_call x1, Pallas kernels, deliver(): pl.pallas_call(body, out_shape=shapes, in_specs=[any_] * count, out_specs...  4.06 us

profile of v1, /device:TPU:0, one launch (start us, length us, event | category | flops | bytes accessed | tf_op | source)
XLA Modules:
  0.0 132.2 jit_solution(8974580031389773545)
XLA Ops:
  0.7 127.4 %shard_map.288 = (bf16[512,1536]{1,0:T(8,128)(2,1)}, bf16[512,1536]{1,0:T(8,128)(2,1)}, f32[1,192]{1,0:T(1,128)}, f32[192,768]{1,0:T(8,128)}, f32[192,768]{1,0:T...) custom-call(bf16[512,1536]{1,0:T(8,128)(2,1)} %refs_0_.1, ...), custom_call_target="tpu_custom_call" | custom-call | tf_op jit(solution)/shard_map/pallas_call | solution.py:1389
  128.0 4.1 %shard_map.289 = (bf16[512,1536]{1,0:T(8,128)(2,1)}, bf16[512,1536]{1,0:T(8,128)(2,1)}, f32[192]{0:T(256)}, f32[192,768]{1,0:T(8,128)}, f32[192,768]{1,0:T(8,128...) custom-call(bf16[512,1536]{1,0:T(8,128)(2,1)} %get-tuple-element.48., ...), custom_call_target="tpu_custom_call" | custom-call | tf_op jit(solution)/shard_map/pallas_call | solution.py:1432

commit v2 on v1

--- a/solution.py
+++ b/solution.py
@@ -925,11 +925,7 @@
         for c in range(nb):
             r.tb[:, c * L : (c + 1) * L] = r.nx[HALO + c * L : HALO + (c + 1) * L, :].T
 
-    transpose_nx()
-    weight_grad(r.tb, r.dgate, r.g_gate, w, nt)
-    rs_send(p_gate, 0)
-    ar_service(5, 7)
-    rs_take(p_out, 0)
+    ar_service(5, 6)
 
     def within_back(c, carry):
         rr, b_rows, c_rows, scores = in_block(c)
@@ -967,12 +963,15 @@
         return carry
 
     lax.fori_loop(0, nb // 2, within_back, 0)
-    rs_take(p_gate, 0)
-    ar_service(7, 8)
+    rs_take(p_out, 0)
+    ar_service(6, 8)
     lax.fori_loop(nb // 2, nb, within_back, 0)
     ar_service(8, 10)
 
     relay_states(bwd_copy, r.bin, behind, 2, p.group)
+    transpose_nx()
+    weight_grad(r.tb, r.dgate, r.g_gate, w, nt)
+    rs_send(p_gate, 0)
     receive_states(bwd_copy, r.bin, behind, lambda k: ok_bwd(k, me))
     for c in range(nb - 1, -1, -1):
         rr = slice(c * L, (c + 1) * L)
@@ -1028,6 +1027,7 @@
         r.dsp[tok : tok + 8, :] = jnp.zeros((8, s2), F32)
 
     ar_service(10, 12)
+    rs_take(p_gate, 0)
 
     up = jnp.where(lane_l >= row_l, 1.0, 0.0).astype(BF)
     below = jnp.where(lane_l < row_l, 1.0, 0.0).astype(BF)

time: 132 us -> 133 us (level)
  no operation moved by 1% of the time
where the time goes in v2:
time: 133 us
  Pallas kernels  132 us (99%)
    pallas_call x1, Pallas kernels, on_device(): pl.pallas_call(functools.partial(kernel, p, names, tuple(small), few_out)...  128 us
    pallas_call x1, Pallas kernels, deliver(): pl.pallas_call(body, out_shape=shapes, in_specs=[any_] * count, out_specs...  4.06 us

profile of v2, /device:TPU:0, one launch (start us, length us, event | category | flops | bytes accessed | tf_op | source)
XLA Modules:
  0.0 132.7 jit_solution(18146601640227803722)
XLA Ops:
  0.7 127.9 %shard_map.288 = (bf16[512,1536]{1,0:T(8,128)(2,1)}, bf16[512,1536]{1,0:T(8,128)(2,1)}, f32[1,192]{1,0:T(1,128)}, f32[192,768]{1,0:T(8,128)}, f32[192,768]{1,0:T...) custom-call(bf16[512,1536]{1,0:T(8,128)(2,1)} %refs_0_.1, ...), custom_call_target="tpu_custom_call" | custom-call | tf_op jit(solution)/shard_map/pallas_call | solution.py:1389
  128.5 4.1 %shard_map.289 = (bf16[512,1536]{1,0:T(8,128)(2,1)}, bf16[512,1536]{1,0:T(8,128)(2,1)}, f32[192]{0:T(256)}, f32[192,768]{1,0:T(8,128)}, f32[192,768]{1,0:T(8,128...) custom-call(bf16[512,1536]{1,0:T(8,128)(2,1)} %get-tuple-element.48., ...), custom_call_target="tpu_custom_call" | custom-call | tf_op jit(solution)/shard_map/pallas_call | solution.py:1432
